TPU v7x, 32 devices: a whole 2x2x4 slice. The times are simulated.
32 devices in a mesh: ty: 8 (over z, core), tx: 4 (over y, x).
Axes of the slice: x: 2, y: 2, z: 4, core: 2. Of those that a mesh axis runs over, the one named last changes fastest.
Arguments:
- image: float32 [4096, 4096], P('ty', 'tx'), may hold values from -6 to 6
- noise: float32 [2, 4096, 4096], P(None, 'ty', 'tx'), may hold values from -6 to 6
- offsets: int32 [2, 2], replicated, may hold values from 1 to 7, as said below
- key_mask: int32 [256, 256], P('ty', 'tx'), may hold values 0 or 1
- gains: float32 [2, 4096, 4096], P(None, ('ty', 'tx')), may hold values from -1 to 1
- observed: float32 [2, 4096, 4096], P(None, ('ty', 'tx')), may hold values from -6 to 6
- vis_weight: float32 [4096, 4096], P(('ty', 'tx')), may hold values from 0.05 to 1
- w_embed: bfloat16 [256, 512], replicated, may hold values from -0.375 to 0.375
- w_qkv: bfloat16 [2, 512, 1536], replicated, as said below
- w_proj: bfloat16 [2, 512, 512], replicated, may hold values from -0.25 to 0.25
- w_up: bfloat16 [2, 512, 2048], replicated, may hold values from -0.25 to 0.25
- w_down: bfloat16 [2, 2048, 512], replicated, may hold values from -0.125 to 0.125
- w_unembed: bfloat16 [512, 256], replicated, may hold values from -0.25 to 0.25
- norm_gains: float32 [2, 2, 512], replicated, may hold values from 0.1 to 1.9
Outputs:
- sampled: float32 [4096, 4096], P('ty', 'tx')
Inputs may be any that keep to these rules, and one draw needn't show every extreme that they name: `offsets`: each entry lies in 1 to 7, and some entry equals 7. `w_qkv`: columns ordered by query, key or value, then head, then feature of the head.
All inputs are finite; a program needn't handle non-finite values. No bound on the sum of `key_mask` on one device may be relied on, other than what follows from the above.
Results may differ from a plain program's by a relative error of at most 0.04.
Values may be sent and summed in bfloat16 or wider, within the bound.
No kernel may reach another device: no remote copies, remote signals or barrier semaphores. Data moves between devices by JAX's collectives and lax.ppermute only.
A program may use at most 192 MiB of HBM per device.

v0:
```python
import math

import jax
import jax.numpy as jnp
from jax import lax
from jax.sharding import PartitionSpec as P

N = 4096
PATCH = 16
WIN = 8
D = 512
HEADS = 8
STEPS = 2


SIGMAS = (0.8, 0.5, 0.3)
STEP_SIZES = (0.9, 0.7)
EPSILON = 1e-05
HIGHEST = lax.Precision.HIGHEST


def from_behind(shard, axis, by):
    size = lax.axis_size(axis)
    return lax.ppermute(shard, axis, [(i, (i + by) % size) for i in range(size)])


def counting(length):
    return jnp.arange(length, dtype=jnp.int32)


def roots(length, outer, inner, sign):
    product = outer[:, None] * inner[None, :] % length
    angle = 2.0 * math.pi / length * product.astype(jnp.float32)
    return (jnp.cos(angle), sign * jnp.sin(angle))


def complex_einsum(form, left, right):
    real = jnp.einsum(form, left[0], right[0], precision=HIGHEST) - jnp.einsum(
        form, left[1], right[1], precision=HIGHEST
    )
    imag = jnp.einsum(form, left[0], right[1], precision=HIGHEST) + jnp.einsum(
        form, left[1], right[0], precision=HIGHEST
    )
    return (real, imag)


def complex_times(left, right):
    return (left[0] * right[0] - left[1] * right[1], left[0] * right[1] + left[1] * right[0])


def along_last(real_part, imag_part, groups, sign):
    rows, length = real_part.shape
    inner = length // groups
    first = roots(groups, counting(groups), counting(groups), sign)
    twist = roots(length, counting(inner), counting(groups), sign)
    second = roots(inner, counting(inner), counting(inner), sign)
    shaped = real_part.reshape(rows, groups, inner)
    if imag_part is None:
        partial_value = (
            jnp.einsum("mab,ka->mbk", shaped, first[0], precision=HIGHEST),
            jnp.einsum("mab,ka->mbk", shaped, first[1], precision=HIGHEST),
        )
    else:
        partial_value = complex_einsum(
            "mab,ka->mbk", (shaped, imag_part.reshape(rows, groups, inner)), first
        )
    partial_value = complex_times(partial_value, twist)
    result = complex_einsum("jb,mbk->mjk", second, partial_value)
    return (result[0].reshape(rows, length), result[1].reshape(rows, length))


def across_groups(pair, lead, trail, sign, keep_imag):
    rows, cols = pair[0].shape
    inner = rows // lead
    width = cols // trail
    groups = lead * trail
    length = groups * inner
    first = roots(groups, counting(groups), counting(groups), sign)
    first = (first[0].reshape(groups, lead, trail), first[1].reshape(groups, lead, trail))
    twist = roots(length, counting(inner), counting(groups), sign)
    second = roots(inner, counting(inner), counting(inner), sign)
    shaped = (
        pair[0].reshape(lead, inner, trail, width),
        pair[1].reshape(lead, inner, trail, width),
    )
    partial_value = complex_einsum("gbhc,kgh->cbk", shaped, first)
    partial_value = complex_times(partial_value, twist)
    if keep_imag:
        result = complex_einsum("jb,cbk->cjk", second, partial_value)
        return (result[0].reshape(width, length), result[1].reshape(width, length))
    real = jnp.einsum("jb,cbk->cjk", second[0], partial_value[0], precision=HIGHEST) - jnp.einsum(
        "jb,cbk->cjk", second[1], partial_value[1], precision=HIGHEST
    )
    return real.reshape(width, length)


def likelihood(tile, gains, observed, vis_weight):
    devices = lax.axis_size("ty") * lax.axis_size("tx")
    slab = lax.all_to_all(
        tile.astype(jnp.bfloat16), "tx", split_axis=0, concat_axis=1, tiled=True
    ).astype(tile.dtype)
    spec_re, spec_im = along_last(slab, None, devices, -1.0)
    moved = (
        lax.all_to_all(
            spec_re.astype(jnp.bfloat16), ("ty", "tx"), split_axis=1, concat_axis=1, tiled=True
        ).astype(spec_re.dtype),
        lax.all_to_all(
            spec_im.astype(jnp.bfloat16), ("ty", "tx"), split_axis=1, concat_axis=1, tiled=True
        ).astype(spec_im.dtype),
    )
    lead = 1
    spectrum = across_groups(moved, lead, devices // lead, -1.0, True)
    spectrum = (spectrum[0] * (1.0 / N), spectrum[1] * (1.0 / N))
    model = complex_times((gains[0], gains[1]), spectrum)
    misfit = (vis_weight * (model[0] - observed[0]), vis_weight * (model[1] - observed[1]))
    back = complex_times((gains[0], -gains[1]), misfit)
    wave_re, wave_im = along_last(back[0], back[1], devices, 1.0)
    returned = (
        lax.all_to_all(
            wave_re.astype(jnp.bfloat16), ("ty", "tx"), split_axis=1, concat_axis=1, tiled=True
        ).astype(wave_re.dtype),
        lax.all_to_all(
            wave_im.astype(jnp.bfloat16), ("ty", "tx"), split_axis=1, concat_axis=1, tiled=True
        ).astype(wave_im.dtype),
    )
    slab_grad = across_groups(returned, lead, devices // lead, 1.0, False) * (1.0 / N)
    return lax.all_to_all(
        slab_grad.astype(jnp.bfloat16), "tx", split_axis=1, concat_axis=0, tiled=True
    ).astype(slab_grad.dtype)


def layer_norm(values, gain):
    centre = jnp.mean(values, axis=-1, keepdims=True)
    shifted = values - centre
    spread = jnp.mean(shifted * shifted, axis=-1, keepdims=True)
    return shifted * lax.rsqrt(spread + EPSILON) * gain


def to_windows(grid):
    rows, cols, feats = grid.shape
    shaped = grid.reshape(rows // WIN, WIN, cols // WIN, WIN, feats).transpose(0, 2, 1, 3, 4)
    return shaped.reshape(rows // WIN * (cols // WIN), WIN * WIN, feats)


def from_windows(windows, rows, cols):
    feats = windows.shape[-1]
    shaped = windows.reshape(rows // WIN, cols // WIN, WIN, WIN, feats).transpose(0, 2, 1, 3, 4)
    return shaped.reshape(rows, cols, feats)


def attention(normed, labels, keep, w_qkv, w_proj):
    rows, cols = (normed.shape[0], normed.shape[1])
    mixed = jnp.dot(normed.reshape(rows * cols, D), w_qkv, preferred_element_type=jnp.float32)
    mixed = to_windows(mixed.astype(jnp.bfloat16).reshape(rows, cols, 3 * D))
    number = mixed.shape[0]
    parts = mixed.reshape(number, WIN * WIN, 3, HEADS, D // HEADS)
    scores = jnp.einsum(
        "wqhe,wkhe->whqk", parts[:, :, 0], parts[:, :, 1], preferred_element_type=jnp.float32
    ) / math.sqrt(D // HEADS)
    label_win = to_windows(labels[:, :, None])[:, :, 0]
    keep_win = to_windows(keep[:, :, None])[:, :, 0]
    same = label_win[:, :, None] == label_win[:, None, :]
    visible = (keep_win[:, None, :] == 1) | jnp.eye(WIN * WIN, dtype=bool)[None]
    allowed = (same & visible)[:, None]
    scores = jnp.where(allowed, scores, -1e30)
    largest = jnp.max(scores, axis=-1, keepdims=True)
    weights = jnp.exp(scores - largest)
    probs = (weights / jnp.sum(weights, axis=-1, keepdims=True)).astype(jnp.bfloat16)
    attended = jnp.einsum(
        "whqk,wkhe->wqhe", probs, parts[:, :, 2], preferred_element_type=jnp.float32
    ).astype(jnp.bfloat16)
    attended = from_windows(attended.reshape(number, WIN * WIN, D), rows, cols)
    projected = jnp.dot(
        attended.reshape(rows * cols, D), w_proj, preferred_element_type=jnp.float32
    )
    return projected.reshape(rows, cols, D)


def swin_block(grid, labels, keep, w_qkv, w_proj, w_up, w_down, gains):
    rows, cols = (grid.shape[0], grid.shape[1])
    flow = grid.astype(jnp.float32)
    normed = layer_norm(flow, gains[0]).astype(jnp.bfloat16)
    flow = flow + attention(normed, labels, keep, w_qkv, w_proj)
    normed = layer_norm(flow, gains[1]).astype(jnp.bfloat16).reshape(rows * cols, D)
    hidden = jax.nn.gelu(
        jnp.dot(normed, w_up, preferred_element_type=jnp.float32), approximate=True
    )
    hidden = hidden.astype(jnp.bfloat16)
    flow = flow + jnp.dot(hidden, w_down, preferred_element_type=jnp.float32).reshape(rows, cols, D)
    return flow.astype(jnp.bfloat16)


def roll_forward(grid, shift_rows, shift_cols):
    rows, cols, feats = grid.shape
    right = from_behind(grid, "tx", -1)
    wide = jnp.concatenate([grid, right], axis=1)
    below = from_behind(wide, "ty", -1)
    whole = jnp.concatenate([wide, below], axis=0)
    anchor = jnp.zeros((), jnp.int32)
    return lax.dynamic_slice(whole, (shift_rows, shift_cols, anchor), (rows, cols, feats))


def roll_back(grid, shift_rows, shift_cols):
    rows, cols, feats = grid.shape
    left = from_behind(grid, "tx", 1)
    wide = jnp.concatenate([left, grid], axis=1)
    above = from_behind(wide, "ty", 1)
    whole = jnp.concatenate([above, wide], axis=0)
    row_start = rows - shift_rows
    col_start = cols - shift_cols
    anchor = jnp.zeros((), jnp.int32)
    return lax.dynamic_slice(whole, (row_start, col_start, anchor), (rows, cols, feats))


def patches_of(picture):
    rows, cols = picture.shape
    shaped = picture.reshape(rows // PATCH, PATCH, cols // PATCH, PATCH).transpose(0, 2, 1, 3)
    return shaped.reshape(rows // PATCH, cols // PATCH, PATCH * PATCH).astype(jnp.bfloat16)


def image_of(pieces):
    rows, cols = (pieces.shape[0], pieces.shape[1])
    shaped = pieces.reshape(rows, cols, PATCH, PATCH).transpose(0, 2, 1, 3)
    return shaped.reshape(rows * PATCH, cols * PATCH)


def region(index, shift):
    side = N // PATCH
    return jnp.where(index < side - WIN, 0, jnp.where(index < side - shift, 1, 2)).astype(jnp.int32)


def per_device(
    image,
    noise,
    offsets,
    key_mask,
    gains,
    observed,
    vis_weight,
    w_embed,
    w_qkv,
    w_proj,
    w_up,
    w_down,
    w_unembed,
    norm_gains,
):
    rows = image.shape[0] // PATCH
    cols = image.shape[1] // PATCH
    plain = jnp.zeros((rows, cols), jnp.int32)
    all_keep = jnp.ones((rows, cols), jnp.int32)
    row_index = lax.axis_index("ty") * rows + counting(rows)
    col_index = lax.axis_index("tx") * cols + counting(cols)
    state = image
    for step in range(STEPS):
        grad = likelihood(state, gains, observed, vis_weight)
        half = state - STEP_SIZES[step] * grad
        patches = patches_of(half)
        tokens = jnp.dot(
            patches.reshape(rows * cols, PATCH * PATCH), w_embed, preferred_element_type=jnp.float32
        )
        tokens = tokens.astype(jnp.bfloat16).reshape(rows, cols, D)
        first = swin_block(
            tokens, plain, key_mask, w_qkv[0], w_proj[0], w_up[0], w_down[0], norm_gains[0]
        )
        shift_rows = offsets[step, 0]
        shift_cols = offsets[step, 1]
        rolled = roll_forward(first, shift_rows, shift_cols)
        regions = (
            3 * region(row_index, shift_rows)[:, None] + region(col_index, shift_cols)[None, :]
        )
        second = swin_block(
            rolled, regions, all_keep, w_qkv[1], w_proj[1], w_up[1], w_down[1], norm_gains[1]
        )
        restored = roll_back(second, shift_rows, shift_cols)
        estimate = jnp.dot(
            restored.reshape(rows * cols, D), w_unembed, preferred_element_type=jnp.float32
        )
        estimate = image_of(estimate.reshape(rows, cols, PATCH * PATCH))
        state = half - SIGMAS[step] * estimate + SIGMAS[step + 1] * noise[step]
    return state


def solution(mesh):
    in_specs = (
        P("ty", "tx"),
        P(None, "ty", "tx"),
        P(),
        P("ty", "tx"),
        P(None, ("ty", "tx"), None),
        P(None, ("ty", "tx"), None),
        P(("ty", "tx"), None),
        P(),
        P(),
        P(),
        P(),
        P(),
        P(),
        P(),
    )
    out_specs = P("ty", "tx")
    return jax.shard_map(
        per_device, mesh=mesh, in_specs=in_specs, out_specs=out_specs, check_vma=False
    )
```

profile of v0, /device:TPU:0, one launch (start us, length us, event | category | flops | bytes accessed | tf_op | source)
XLA Modules:
  0.0 1389.9 jit_solution(3640738433023341445)
XLA Ops:
  8.0 13.5 all-to-all-done
  49.8 16.1 %all-to-all-done.1 = bf16[128,32,128]{2,0,1:T(8,128)(2,1)S(1)} async-done(((bf16[128,32,128]{2,0,1:T(8,128)(2,1)}), bf16[128,32,128]{2,0,1:T(8,128)(2,1)S(1)}, u32[]{:S(2)}, u32[]{:S(2)}) %all-to-all-start.1) | async-done | bytes 1048608 | tf_op jit(solution)/shard_map/all_to_all | solution.py:104
  176.4 17.5 %all-to-all-done.3 = bf16[128,32,128]{2,0,1:T(8,128)(2,1)S(1)} async-done(((bf16[128,32,128]{2,0,1:T(8,128)(2,1)}), bf16[128,32,128]{2,0,1:T(8,128)(2,1)S(1)}, u32[]{:S(2)}, u32[]{:S(2)}) %all-to-all-start.3) | async-done | bytes 1048608 | tf_op jit(solution)/shard_map/all_to_all | solution.py:119
  201.9 22.0 %all-to-all-done.4 = bf16[128,32,128]{2,0,1:T(8,128)(2,1)} async-done(((bf16[128,32,128]{2,0,1:T(8,128)(2,1)}), bf16[128,32,128]{2,0,1:T(8,128)(2,1)}, u32[]{:S(2)}, u32[]{:S(2)}) %all-to-all-start.4) | async-done | bytes 1048608 | tf_op jit(solution)/shard_map/all_to_all | solution.py:122
  243.7 12.0 all-to-all-done.5
  262.1 8.3 convert_element_type.557
  289.1 16.3 %reshape_reshape.43 = bf16[32,64,3,8,64]{4,3,2,1,0:T(8,128)(2,1)} reshape(bf16[4,8,8,8,1536]{4,3,2,1,0:T(8,128)(2,1)} %bitcast.649) | data formatting | bytes 12582912 | tf_op jit(solution)/shard_map/reshape;reshape | solution.py:156
  305.4 9.0 fusion.736
  372.5 45.4 %collective-permute-done = bf16[32,64,512]{2,1,0:T(8,128)(2,1)S(1)} collective-permute-done((bf16[32,64,512]{2,1,0:T(8,128)(2,1)S(1)}, bf16[32,64,512]{2,1,0:T(8,128)(2,1)S(1)}, u32[]{:S(2)}, u32[]{:S(2)}) %collective-permute-start) | collective-permute-done | bytes 2097184 | tf_op jit(solution)/shard_map/ppermute | solution.py:24
  429.7 37.3 %collective-permute-done.1 = bf16[32,128,512]{2,1,0:T(8,128)(2,1)} collective-permute-done((bf16[32,128,512]{2,1,0:T(8,128)(2,1)}, bf16[32,128,512]{2,1,0:T(8,128)(2,1)}, u32[]{:S(2)}, u32[]{:S(2)}) %collective-permute-start.1) | collective-permute-done | bytes 4194336 | tf_op jit(solution)/shard_map/ppermute | solution.py:24
  481.0 16.3 %reshape_reshape.46 = bf16[32,64,3,8,64]{4,3,2,1,0:T(8,128)(2,1)} reshape(bf16[4,8,8,8,1536]{4,3,2,1,0:T(8,128)(2,1)} %bitcast.650) | data formatting | bytes 12582912 | tf_op jit(solution)/shard_map/reshape;reshape | solution.py:156
  497.3 9.0 fusion.735
  565.0 47.2 %collective-permute-done.2 = bf16[32,64,512]{2,1,0:T(8,128)(2,1)S(1)} collective-permute-done((bf16[32,64,512]{2,1,0:T(8,128)(2,1)S(1)}, bf16[32,64,512]{2,1,0:T(8,128)(2,1)S(1)}, u32[]{:S(2)}, u32[]{:S(2)}) %collective-permute-start.2) | collective-permute-done | bytes 2097184 | tf_op jit(solution)/shard_map/ppermute | solution.py:24
  617.6 47.3 %collective-permute-done.3 = bf16[32,128,512]{2,1,0:T(8,128)(2,1)} collective-permute-done((bf16[32,128,512]{2,1,0:T(8,128)(2,1)}, bf16[32,128,512]{2,1,0:T(8,128)(2,1)}, u32[]{:S(2)}, u32[]{:S(2)}) %collective-permute-start.3) | collective-permute-done | bytes 4194336 | tf_op jit(solution)/shard_map/ppermute | solution.py:24
  671.2 10.5 copy.380
  681.7 15.4 %mul.1817 = f32[512,1024]{1,0:T(8,128)} reshape(f32[32,16,64,16]{3,2,1,0:T(8,128)} %copy.380) | data formatting | bytes 4194304 | tf_op jit(solution)/shard_map/mul | solution.py:280
  702.3 13.0 all_to_all.100
  741.4 16.1 %all-to-all-done.7 = bf16[128,32,128]{2,0,1:T(8,128)(2,1)S(1)} async-done(((bf16[128,32,128]{2,0,1:T(8,128)(2,1)}), bf16[128,32,128]{2,0,1:T(8,128)(2,1)S(1)}, u32[]{:S(2)}, u32[]{:S(2)}) %all-to-all-start.7) | async-done | bytes 1048608 | tf_op jit(solution)/shard_map/all_to_all | solution.py:104
  765.4 22.0 %all-to-all-done.8 = bf16[128,32,128]{2,0,1:T(8,128)(2,1)} async-done(((bf16[128,32,128]{2,0,1:T(8,128)(2,1)}), bf16[128,32,128]{2,0,1:T(8,128)(2,1)}, u32[]{:S(2)}, u32[]{:S(2)}) %all-to-all-start.8) | async-done | bytes 1048608 | tf_op jit(solution)/shard_map/all_to_all | solution.py:107
  859.8 17.5 %all-to-all-done.9 = bf16[128,32,128]{2,0,1:T(8,128)(2,1)S(1)} async-done(((bf16[128,32,128]{2,0,1:T(8,128)(2,1)}), bf16[128,32,128]{2,0,1:T(8,128)(2,1)S(1)}, u32[]{:S(2)}, u32[]{:S(2)}) %all-to-all-start.9) | async-done | bytes 1048608 | tf_op jit(solution)/shard_map/all_to_all | solution.py:119
  885.3 22.0 %all-to-all-done.10 = bf16[128,32,128]{2,0,1:T(8,128)(2,1)} async-done(((bf16[128,32,128]{2,0,1:T(8,128)(2,1)}), bf16[128,32,128]{2,0,1:T(8,128)(2,1)}, u32[]{:S(2)}, u32[]{:S(2)}) %all-to-all-start.10) | async-done | bytes 1048608 | tf_op jit(solution)/shard_map/all_to_all | solution.py:122
  920.4 17.2 %all_to_all.101 = bf16[128,4,1024]{0,2,1:T(8,128)(2,1)S(1)} all-to-all(bf16[128,4,1024]{0,2,1:T(8,128)(2,1)S(1)} %bitcast.681), channel_id=1, replica_groups=mesh['ty'=8,'tx'=4] {'tx'}, dimensions={1} | all-to-all | bytes 2097152 | tf_op jit(solution)/shard_map/all_to_all | solution.py:127
  970.7 16.3 %reshape_reshape.49 = bf16[32,64,3,8,64]{4,3,2,1,0:T(8,128)(2,1)} reshape(bf16[4,8,8,8,1536]{4,3,2,1,0:T(8,128)(2,1)} %bitcast.651) | data formatting | bytes 12582912 | tf_op jit(solution)/shard_map/reshape;reshape | solution.py:156
  1000.0 12.1 fusion.745
  1060.6 44.3 %collective-permute-done.4 = bf16[32,64,512]{2,1,0:T(8,128)(2,1)S(1)} collective-permute-done((bf16[32,64,512]{2,1,0:T(8,128)(2,1)S(1)}, bf16[32,64,512]{2,1,0:T(8,128)(2,1)S(1)}, u32[]{:S(2)}, u32[]{:S(2)}) %collective-permute-start.4) | collective-permute-done | bytes 2097184 | tf_op jit(solution)/shard_map/ppermute | solution.py:24
  1112.6 41.3 %collective-permute-done.5 = bf16[32,128,512]{2,1,0:T(8,128)(2,1)} collective-permute-done((bf16[32,128,512]{2,1,0:T(8,128)(2,1)}, bf16[32,128,512]{2,1,0:T(8,128)(2,1)}, u32[]{:S(2)}, u32[]{:S(2)}) %collective-permute-start.5) | collective-permute-done | bytes 4194336 | tf_op jit(solution)/shard_map/ppermute | solution.py:24
  1168.1 16.3 %reshape_reshape.52 = bf16[32,64,3,8,64]{4,3,2,1,0:T(8,128)(2,1)} reshape(bf16[4,8,8,8,1536]{4,3,2,1,0:T(8,128)(2,1)} %bitcast.652) | data formatting | bytes 12582912 | tf_op jit(solution)/shard_map/reshape;reshape | solution.py:156
  1184.4 9.0 fusion.733
  1252.0 47.2 %collective-permute-done.6 = bf16[32,64,512]{2,1,0:T(8,128)(2,1)S(1)} collective-permute-done((bf16[32,64,512]{2,1,0:T(8,128)(2,1)S(1)}, bf16[32,64,512]{2,1,0:T(8,128)(2,1)S(1)}, u32[]{:S(2)}, u32[]{:S(2)}) %collective-permute-start.6) | collective-permute-done | bytes 2097184 | tf_op jit(solution)/shard_map/ppermute | solution.py:24
  1304.4 47.5 %collective-permute-done.7 = bf16[32,128,512]{2,1,0:T(8,128)(2,1)} collective-permute-done((bf16[32,128,512]{2,1,0:T(8,128)(2,1)}, bf16[32,128,512]{2,1,0:T(8,128)(2,1)}, u32[]{:S(2)}, u32[]{:S(2)}) %collective-permute-start.7) | collective-permute-done | bytes 4194336 | tf_op jit(solution)/shard_map/ppermute | solution.py:24
  1358.2 10.7 copy.445
  1368.9 15.4 %mul.1884 = f32[512,1024]{1,0:T(8,128)} reshape(f32[32,16,64,16]{3,2,1,0:T(8,128)} %copy.445) | data formatting | bytes 4194304 | tf_op jit(solution)/shard_map/mul | solution.py:280
  (407 shorter events, 661.4 us)
Async XLA Ops:
  0.0 279.9 %copy-start = (bf16[256,512]{1,0:T(8,128)(2,1)S(1)}, bf16[256,512]{1,0:T(8,128)(2,1)}, u32[]{:S(2)}) copy-start(bf16[256,512]{1,0:T(8,128)(2,1)} %param.21) | copy-start | bytes 786436
  2.8 18.8 %all-to-all-start = ((bf16[4,128,1024]{2,1,0:T(8,128)(2,1)}), bf16[4,128,1024]{2,1,0:T(8,128)(2,1)S(1)}, u32[]{:S(2)}, u32[]{:S(2)}) async-start(bf16[4,128,1024]{2,1,0:T(8,128)(2,1)} %bitcast.2), calls=%async_computation | async-start | bytes 2097152 | tf_op jit(solution)/shard_map/all_to_all | solution.py:99
  8.0 97.2 %copy-start.49 = (f32[128,32]{0,1:T(8,128)}, f32[128,32]{0,1:T(8,128)S(1)}, u32[]{:S(2)}) copy-start(f32[128,32]{0,1:T(8,128)S(1)} %get-tuple-element.77) | copy-start | bytes 49156
  8.0 219.3 %copy-start.45 = (f32[128,32]{0,1:T(8,128)}, f32[128,32]{0,1:T(8,128)S(1)}, u32[]{:S(2)}) copy-start(f32[128,32]{0,1:T(8,128)S(1)} %get-tuple-element.78) | copy-start | bytes 49156
  34.3 31.6 %all-to-all-start.1 = ((bf16[128,32,128]{2,0,1:T(8,128)(2,1)}), bf16[128,32,128]{2,0,1:T(8,128)(2,1)S(1)}, u32[]{:S(2)}, u32[]{:S(2)}) async-start(bf16[128,32,128]{2,0,1:T(8,128)(2,1)} %copy.315), calls=%async_computation.1 | async-start | bytes 2097152 | tf_op jit(solution)/shard_map/all_to_all | solution.py:104
  65.8 34.0 %all-to-all-start.2 = ((bf16[128,32,128]{2,0,1:T(8,128)(2,1)}), bf16[128,32,128]{2,0,1:T(8,128)(2,1)}, u32[]{:S(2)}, u32[]{:S(2)}) async-start(bf16[128,32,128]{2,0,1:T(8,128)(2,1)} %copy.320), calls=%async_computation.2 | async-start | bytes 2097152 | tf_op jit(solution)/shard_map/all_to_all | solution.py:107
  76.0 55.1 %copy-start.1 = (f32[1,128,4096]{1,2,0:T(8,128)}, f32[1,128,4096]{1,2,0:T(8,128)S(1)}, u32[]{:S(2)}) copy-start(f32[1,128,4096]{1,2,0:T(8,128)S(1)} %copy.500) | copy-start | bytes 6291460
  93.1 134.2 %copy-start.47 = (f32[128,32]{0,1:T(8,128)}, f32[128,32]{0,1:T(8,128)S(1)}, u32[]{:S(2)}) copy-start(f32[128,32]{0,1:T(8,128)S(1)} %fusion.438) | copy-start | bytes 49156
  161.8 32.2 %all-to-all-start.3 = ((bf16[128,32,128]{2,0,1:T(8,128)(2,1)}), bf16[128,32,128]{2,0,1:T(8,128)(2,1)S(1)}, u32[]{:S(2)}, u32[]{:S(2)}) async-start(bf16[128,32,128]{2,0,1:T(8,128)(2,1)} %copy.346), calls=%async_computation.3 | async-start | bytes 2097152 | tf_op jit(solution)/shard_map/all_to_all | solution.py:119
  194.0 30.0 %all-to-all-start.4 = ((bf16[128,32,128]{2,0,1:T(8,128)(2,1)}), bf16[128,32,128]{2,0,1:T(8,128)(2,1)}, u32[]{:S(2)}, u32[]{:S(2)}) async-start(bf16[128,32,128]{2,0,1:T(8,128)(2,1)} %copy.351), calls=%async_computation.4 | async-start | bytes 2097152 | tf_op jit(solution)/shard_map/all_to_all | solution.py:122
  237.8 17.9 %all-to-all-start.5 = ((bf16[128,4,1024]{0,2,1:T(8,128)(2,1)}), bf16[128,4,1024]{0,2,1:T(8,128)(2,1)S(1)}, u32[]{:S(2)}, u32[]{:S(2)}) async-start(bf16[128,4,1024]{0,2,1:T(8,128)(2,1)} %bitcast.33), calls=%async_computation.5 | async-start | bytes 2097152 | tf_op jit(solution)/shard_map/all_to_all | solution.py:127
  242.6 113.4 %copy-start.60 = (f32[1,1,512]{2,1,0:T(1,128)}, f32[1,1,512]{2,1,0:T(1,128)S(1)}, u32[]{:S(2)}) copy-start(f32[1,1,512]{2,1,0:T(1,128)S(1)} %get-tuple-element.50) | copy-start | bytes 6148
  242.7 229.3 %copy-start.58 = (f32[1,1,512]{2,1,0:T(1,128)}, f32[1,1,512]{2,1,0:T(1,128)S(1)}, u32[]{:S(2)}) copy-start(f32[1,1,512]{2,1,0:T(1,128)S(1)} %get-tuple-element.52) | copy-start | bytes 6148
  371.1 49.5 %copy-start.33 = (bf16[32,64,512]{2,1,0:T(8,128)(2,1)}, bf16[32,64,512]{2,1,0:T(8,128)(2,1)S(1)}, u32[]{:S(2)}) copy-start(bf16[32,64,512]{2,1,0:T(8,128)(2,1)S(1)} %add_convert_fusion.3) | copy-start | bytes 6291460
  371.1 49.5 %copy-start.66 = (s32[2,2]{1,0:T(2,128)S(1)}, s32[2,2]{1,0:T(2,128)}, u32[]{:S(2)}) copy-start(s32[2,2]{1,0:T(2,128)} %param.16) | copy-start | bytes 52
  371.1 46.8 %collective-permute-start = (bf16[32,64,512]{2,1,0:T(8,128)(2,1)S(1)}, bf16[32,64,512]{2,1,0:T(8,128)(2,1)S(1)}, u32[]{:S(2)}, u32[]{:S(2)}) collective-permute-start(bf16[32,64,512]{2,1,0:T(8,128)(2,1)S(1)} %add_convert_fusion.3), channel_id=1, source_target_pairs={{0,3},{1,0},{2,1},{3,2},{4,7},{5,4},{6,5},{7,6},{8,11},{9,8},{10,9... | collective-permute-start | bytes 6291464 | tf_op jit(solution)/shard_map/ppermute | solution.py:24
  420.6 46.3 %collective-permute-start.1 = (bf16[32,128,512]{2,1,0:T(8,128)(2,1)}, bf16[32,128,512]{2,1,0:T(8,128)(2,1)}, u32[]{:S(2)}, u32[]{:S(2)}) collective-permute-start(bf16[32,128,512]{2,1,0:T(8,128)(2,1)} %pad_maximum_fusion), channel_id=1, source_target_pairs={{0,28},{4,0},{8,4},{12,8},{16,12},{20,16},{24,20},{28,24},{1,29},{... | collective-permute-start | bytes 12582920 | tf_op jit(solution)/shard_map/ppermute | solution.py:24
  562.7 54.7 %copy-start.53 = (bf16[512,256]{1,0:T(8,128)(2,1)S(1)}, bf16[512,256]{1,0:T(8,128)(2,1)}, u32[]{:S(2)}) copy-start(bf16[512,256]{1,0:T(8,128)(2,1)} %param.26) | copy-start | bytes 786436
  562.8 49.5 %collective-permute-start.2 = (bf16[32,64,512]{2,1,0:T(8,128)(2,1)S(1)}, bf16[32,64,512]{2,1,0:T(8,128)(2,1)S(1)}, u32[]{:S(2)}, u32[]{:S(2)}) collective-permute-start(bf16[32,64,512]{2,1,0:T(8,128)(2,1)S(1)} %add_convert_fusion.2), channel_id=1, source_target_pairs={{0,1},{1,2},{2,3},{3,0},{4,5},{5,6},{6,7},{7,4},{8,9},{9,10},{10,1... | collective-permute-start | bytes 6291464 | tf_op jit(solution)/shard_map/ppermute | solution.py:24
  614.9 50.0 %collective-permute-start.3 = (bf16[32,128,512]{2,1,0:T(8,128)(2,1)}, bf16[32,128,512]{2,1,0:T(8,128)(2,1)}, u32[]{:S(2)}, u32[]{:S(2)}) collective-permute-start(bf16[32,128,512]{2,1,0:T(8,128)(2,1)} %pad_maximum_fusion.1), channel_id=1, source_target_pairs={{0,4},{4,8},{8,12},{12,16},{16,20},{20,24},{24,28},{28,0},{1,5},{5... | collective-permute-start | bytes 12582920 | tf_op jit(solution)/shard_map/ppermute | solution.py:24
  617.6 53.7 %copy-start.43 = (bf16[512,256]{0,1:T(8,128)(2,1)}, bf16[512,256]{0,1:T(8,128)(2,1)S(1)}, u32[]{:S(2)}) copy-start(bf16[512,256]{0,1:T(8,128)(2,1)S(1)} %copy.379) | copy-start | bytes 786436
  728.0 29.5 %all-to-all-start.7 = ((bf16[128,32,128]{2,0,1:T(8,128)(2,1)}), bf16[128,32,128]{2,0,1:T(8,128)(2,1)S(1)}, u32[]{:S(2)}, u32[]{:S(2)}) async-start(bf16[128,32,128]{2,0,1:T(8,128)(2,1)} %copy.385), calls=%async_computation.7 | async-start | bytes 2097152 | tf_op jit(solution)/shard_map/all_to_all | solution.py:104
  757.5 29.9 %all-to-all-start.8 = ((bf16[128,32,128]{2,0,1:T(8,128)(2,1)}), bf16[128,32,128]{2,0,1:T(8,128)(2,1)}, u32[]{:S(2)}, u32[]{:S(2)}) async-start(bf16[128,32,128]{2,0,1:T(8,128)(2,1)} %copy.390), calls=%async_computation.8 | async-start | bytes 2097152 | tf_op jit(solution)/shard_map/all_to_all | solution.py:107
  847.5 29.9 %all-to-all-start.9 = ((bf16[128,32,128]{2,0,1:T(8,128)(2,1)}), bf16[128,32,128]{2,0,1:T(8,128)(2,1)S(1)}, u32[]{:S(2)}, u32[]{:S(2)}) async-start(bf16[128,32,128]{2,0,1:T(8,128)(2,1)} %copy.413), calls=%async_computation.9 | async-start | bytes 2097152 | tf_op jit(solution)/shard_map/all_to_all | solution.py:119
  877.4 30.0 %all-to-all-start.10 = ((bf16[128,32,128]{2,0,1:T(8,128)(2,1)}), bf16[128,32,128]{2,0,1:T(8,128)(2,1)}, u32[]{:S(2)}, u32[]{:S(2)}) async-start(bf16[128,32,128]{2,0,1:T(8,128)(2,1)} %copy.418), calls=%async_computation.10 | async-start | bytes 2097152 | tf_op jit(solution)/shard_map/all_to_all | solution.py:122
  1059.6 50.5 %copy-start.63 = (s32[8,8]{1,0:T(8,128)S(1)}, s32[8,8]{1,0:T(8,128)}, u32[]{:S(2)}) copy-start(s32[8,8]{1,0:T(8,128)} %get-tuple-element.79) | copy-start | bytes 772
  1059.6 50.5 %copy-start.64 = (s32[4,8]{1,0:T(4,128)S(1)}, s32[4,8]{1,0:T(4,128)}, u32[]{:S(2)}) copy-start(s32[4,8]{1,0:T(4,128)} %get-tuple-element.81) | copy-start | bytes 388
  1059.6 45.3 %collective-permute-start.4 = (bf16[32,64,512]{2,1,0:T(8,128)(2,1)S(1)}, bf16[32,64,512]{2,1,0:T(8,128)(2,1)S(1)}, u32[]{:S(2)}, u32[]{:S(2)}) collective-permute-start(bf16[32,64,512]{2,1,0:T(8,128)(2,1)S(1)} %add_convert_fusion.1), channel_id=1, source_target_pairs={{0,3},{1,0},{2,1},{3,2},{4,7},{5,4},{6,5},{7,6},{8,11},{9,8},{10,9... | collective-permute-start | bytes 6291464 | tf_op jit(solution)/shard_map/ppermute | solution.py:24
  1107.6 46.3 %collective-permute-start.5 = (bf16[32,128,512]{2,1,0:T(8,128)(2,1)}, bf16[32,128,512]{2,1,0:T(8,128)(2,1)}, u32[]{:S(2)}, u32[]{:S(2)}) collective-permute-start(bf16[32,128,512]{2,1,0:T(8,128)(2,1)} %pad_maximum_fusion.2), channel_id=1, source_target_pairs={{0,28},{4,0},{8,4},{12,8},{16,12},{20,16},{24,20},{28,24},{1,29},{... | collective-permute-start | bytes 12582920 | tf_op jit(solution)/shard_map/ppermute | solution.py:24
  1249.8 102.1 %copy-start.44 = (bf16[512,256]{0,1:T(8,128)(2,1)S(1)}, bf16[512,256]{0,1:T(8,128)(2,1)}, u32[]{:S(2)}) copy-start(bf16[512,256]{0,1:T(8,128)(2,1)} %copy-done.43) | copy-start | bytes 786436
  1249.8 49.4 %collective-permute-start.6 = (bf16[32,64,512]{2,1,0:T(8,128)(2,1)S(1)}, bf16[32,64,512]{2,1,0:T(8,128)(2,1)S(1)}, u32[]{:S(2)}, u32[]{:S(2)}) collective-permute-start(bf16[32,64,512]{2,1,0:T(8,128)(2,1)S(1)} %add_convert_fusion), channel_id=1, source_target_pairs={{0,1},{1,2},{2,3},{3,0},{4,5},{5,6},{6,7},{7,4},{8,9},{9,10},{10,1... | collective-permute-start | bytes 6291464 | tf_op jit(solution)/shard_map/ppermute | solution.py:24
  1301.9 50.0 %collective-permute-start.7 = (bf16[32,128,512]{2,1,0:T(8,128)(2,1)}, bf16[32,128,512]{2,1,0:T(8,128)(2,1)}, u32[]{:S(2)}, u32[]{:S(2)}) collective-permute-start(bf16[32,128,512]{2,1,0:T(8,128)(2,1)} %pad_maximum_fusion.3), channel_id=1, source_target_pairs={{0,4},{4,8},{8,12},{12,16},{16,20},{20,24},{24,28},{28,0},{1,5},{5... | collective-permute-start | bytes 12582920 | tf_op jit(solution)/shard_map/ppermute | solution.py:24
  (67 other events, 351.2 us)
where the time goes:
time: 1400 us; the launch traced here: 1390 us
  waiting for transfers between devices  516 us (37%)
  local copies, waits for them, and re-layouts  383 us (27%)
  matrix products  296 us (21%)
  other arithmetic  100 us (7%)
  starting transfers between devices  47.5 us (3%)
  blocking collectives  30.3 us (2%)
  between operations  17.1 us (1%)
    ppermute x8, waiting for transfers between devices, from_behind(): lax.ppermute(shard, axis, [(i, (i + by) % size) for i in range(size)])  358 us
    another operation x4, local copies, waits for them, and re-layouts, attention(): parts = mixed.reshape(number, WIN * WIN, 3, HEADS, D // HEADS)  65.2 us
    mul x4, local copies, waits for them, and re-layouts, per_device(): state = half - SIGMAS[step] * estimate + SIGMAS[step + 1] * noise[step]  52 us
    unnamed x172, local copies, waits for them, and re-layouts  49.6 us
    all_to_all x2, waiting for transfers between devices, likelihood(): lax.all_to_all(wave_im.astype(jnp.bfloat16), ('ty', 'tx'), split_axis=1,...  44 us
    dot_general x12, matrix products, complex_einsum(): jnp.einsum(form, left[0], right[1], precision=HIGHEST)  39.3 us
    convert_element_type x6, local copies, waits for them, and re-layouts, patches_of(): shaped.reshape(rows // PATCH, cols // PATCH, PATCH * PATCH)  35.6 us
    all_to_all x2, waiting for transfers between devices, likelihood(): lax.all_to_all(wave_re.astype(jnp.bfloat16), ('ty', 'tx'), split_axis=1,...  35.1 us
  transfers between devices with their start and end apart: 18, of which 17 were waited for; matrix products, arithmetic and copies ran while one was open for 6% of the time, Pallas kernels for 0%

commit v1 on v0

v1 whole, which is shorter than its diff:
```python
import functools
import math

import jax
import jax.numpy as jnp
import ml_dtypes
import numpy as np
from jax import lax
from jax.experimental import pallas as pl
from jax.experimental.pallas import tpu as pltpu
from jax.sharding import PartitionSpec as P

N = 4096
PATCH = 16
PIXELS = PATCH * PATCH
WIN = 8
D = 512
HEADS = 8
STEPS = 2
SPAN = WIN * WIN
TOK = N // PATCH

SIGMAS = (0.8, 0.5, 0.3)
STEP_SIZES = (0.9, 0.7)
EPSILON = 1e-05
HIGHEST = lax.Precision.HIGHEST
BF16 = jnp.bfloat16
F32 = jnp.float32
VMEM_LIMIT = 56 * 1024 * 1024
PARAMS = pltpu.CompilerParams(vmem_limit_bytes=VMEM_LIMIT)
TN = (((0,), (0,)), ((), ()))
NT = (((1,), (1,)), ((), ()))
NN = (((1,), (0,)), ((), ()))


def mm(left, right, dims=NN):
    return lax.dot_general(left, right, dims, preferred_element_type=F32)


def counting(length):
    return jnp.arange(length, dtype=jnp.int32)


def roots(length, outer, inner, sign):
    product = outer[:, None] * inner[None, :] % length
    angle = 2.0 * math.pi / length * product.astype(F32)
    return (jnp.cos(angle), sign * jnp.sin(angle))


def complex_einsum(form, left, right):
    real = jnp.einsum(form, left[0], right[0], precision=HIGHEST) - jnp.einsum(
        form, left[1], right[1], precision=HIGHEST
    )
    imag = jnp.einsum(form, left[0], right[1], precision=HIGHEST) + jnp.einsum(
        form, left[1], right[0], precision=HIGHEST
    )
    return (real, imag)


def complex_times(left, right):
    return (left[0] * right[0] - left[1] * right[1], left[0] * right[1] + left[1] * right[0])


def along_last(real_part, imag_part, groups, sign):
    rows, length = real_part.shape
    inner = length // groups
    first = roots(groups, counting(groups), counting(groups), sign)
    twist = roots(length, counting(inner), counting(groups), sign)
    second = roots(inner, counting(inner), counting(inner), sign)
    shaped = real_part.reshape(rows, groups, inner)
    if imag_part is None:
        partial_value = (
            jnp.einsum("mab,ka->mbk", shaped, first[0], precision=HIGHEST),
            jnp.einsum("mab,ka->mbk", shaped, first[1], precision=HIGHEST),
        )
    else:
        partial_value = complex_einsum(
            "mab,ka->mbk", (shaped, imag_part.reshape(rows, groups, inner)), first
        )
    partial_value = complex_times(partial_value, twist)
    result = complex_einsum("jb,mbk->mjk", second, partial_value)
    return (result[0].reshape(rows, length), result[1].reshape(rows, length))


def across_groups(pair, groups, sign):
    inner, cols = pair[0].shape
    width = cols // groups
    length = groups * inner
    first = roots(groups, counting(groups), counting(groups), sign)
    twist = roots(length, counting(inner), counting(groups), sign)
    second = roots(inner, counting(inner), counting(inner), sign)
    shaped = (pair[0].reshape(inner, groups, width), pair[1].reshape(inner, groups, width))
    partial_value = complex_einsum("bhc,kh->cbk", shaped, first)
    partial_value = complex_times(partial_value, twist)
    result = complex_einsum("jb,cbk->cjk", second, partial_value)
    return (result[0].reshape(width, length), result[1].reshape(width, length))


def exchange_pair(pair):
    return tuple(
        lax.all_to_all(
            part.astype(BF16), ("ty", "tx"), split_axis=1, concat_axis=1, tiled=True
        ).astype(F32)
        for part in pair
    )


def plain_gradient(tile, gains, observed, vis_weight):
    devices = lax.axis_size("ty") * lax.axis_size("tx")
    slab = lax.all_to_all(tile.astype(BF16), "tx", split_axis=0, concat_axis=1, tiled=True)
    moved = exchange_pair(along_last(slab.astype(F32), None, devices, -1.0))
    spectrum = across_groups(moved, devices, -1.0)
    spectrum = (spectrum[0] * (1.0 / N), spectrum[1] * (1.0 / N))
    model = complex_times((gains[0], gains[1]), spectrum)
    misfit = (vis_weight * (model[0] - observed[0]), vis_weight * (model[1] - observed[1]))
    back = complex_times((gains[0], -gains[1]), misfit)
    returned = exchange_pair(along_last(back[0], back[1], devices, 1.0))
    slab_grad = across_groups(returned, devices, 1.0)[0] * (1.0 / N)
    return lax.all_to_all(slab_grad.astype(BF16), "tx", split_axis=1, concat_axis=0, tiled=True)


def embed_complex(angle, row_axis, col_axis):
    cos, sin = np.cos(angle), np.sin(angle)
    top = np.stack([cos, sin], axis=col_axis)
    bottom = np.stack([-sin, cos], axis=col_axis)
    return np.stack([top, bottom], axis=row_axis)


def wheel(length, product):
    return 2.0 * math.pi / length * (product % length)


@functools.lru_cache(maxsize=None)
def row_constants():
    k = np.arange(TOK)
    angle = wheel(TOK, k[:, None] * k[None, :])
    first = np.concatenate([np.cos(angle), -np.sin(angle)], axis=1)
    b = np.tile(np.arange(PATCH), PATCH)
    angle = wheel(N, b[:, None] * k[None, :])
    twist = np.stack([np.cos(angle), -np.sin(angle)])
    p = np.arange(PATCH)
    small = embed_complex(wheel(PATCH, p[:, None] * p[None, :]), 1, 1)
    second = np.einsum("kpqb,xy->kpxqyb", small, np.eye(PATCH)).reshape(2 * PIXELS, 2 * PIXELS)
    return (
        first.astype(ml_dtypes.bfloat16),
        twist.astype(np.float32),
        second.astype(ml_dtypes.bfloat16),
        np.ascontiguousarray(second.T).astype(ml_dtypes.bfloat16),
    )


@functools.lru_cache(maxsize=None)
def column_constants(devices, rows):
    s = np.arange(devices)
    small = embed_complex(wheel(devices, s[:, None] * s[None, :]), 1, 2)
    wide = devices * 2 * PATCH
    outer = np.einsum("qpsr,xy->qpxsry", small, np.eye(PATCH)).reshape(wide, wide)
    kr = s[:, None] + devices * np.arange(rows)[None, :]
    angle = wheel(N, kr[:, :, None] * np.arange(rows)[None, None, :])
    inner = embed_complex(angle, 1, 2).reshape(devices, 2 * rows, 2 * rows) / N
    return tuple(
        np.ascontiguousarray(value).astype(ml_dtypes.bfloat16)
        for value in (outer, outer.T, inner, inner.transpose(0, 2, 1))
    )


def row_forward(x_ref, first_ref, twist_ref, second_ref, out_ref):
    count = x_ref.shape[1]

    def step(i, carry):
        band = x_ref[:, i].reshape(TOK, PIXELS)
        mixed = mm(band, first_ref[...], TN)
        real, imag = mixed[:, :TOK], mixed[:, TOK:]
        tr, ti = twist_ref[0], twist_ref[1]
        turned = jnp.concatenate(
            [(real * tr - imag * ti).astype(BF16), (real * ti + imag * tr).astype(BF16)], axis=0
        )
        result = mm(second_ref[...], turned).astype(BF16).reshape(PATCH, 2, PATCH, TOK)
        half = TOK // 2
        rows = pl.ds(pl.multiple_of(i * PATCH, PATCH), PATCH)
        out_ref[:, 0, :, rows, :] = result[..., :half]
        out_ref[:, 1, :, rows, :] = result[..., half:]
        return carry

    lax.fori_loop(0, count, step, 0)


def row_inverse(v_ref, first_ref, twist_ref, second_ref, out_ref):
    parts, count, cols, _ = out_ref.shape

    def step(i, carry):
        rows = pl.ds(pl.multiple_of(i * PATCH, PATCH), PATCH)
        wide = jnp.concatenate(
            [
                v_ref[:, 0, :, rows, :].reshape(2 * PIXELS, TOK // 2),
                v_ref[:, 1, :, rows, :].reshape(2 * PIXELS, TOK // 2),
            ],
            axis=1,
        )
        mixed = mm(second_ref[...], wide)
        real, imag = mixed[:PIXELS], mixed[PIXELS:]
        tr, ti = twist_ref[0], twist_ref[1]
        turned = jnp.concatenate(
            [(real * tr + imag * ti).astype(BF16), (imag * tr - real * ti).astype(BF16)], axis=1
        )
        result = mm(first_ref[...], turned, NT).astype(BF16)
        out_ref[:, i] = result.reshape(parts, cols, PIXELS)
        return carry

    lax.fori_loop(0, count, step, 0)


def column_both(
    x_ref, scale_ref, data_ref, outer_ref, outer_t_ref, inner_ref, inner_t_ref, out_ref, mid_ref
):
    devices, _, rows, width = x_ref.shape
    wide = devices * 2 * PATCH

    def turn(source, target, matrix):
        for pair in range(rows // (2 * PATCH)):
            first = slice(pair * 2 * PATCH, pair * 2 * PATCH + PATCH)
            second = slice(pair * 2 * PATCH + PATCH, (pair + 1) * 2 * PATCH)
            both = jnp.concatenate(
                [
                    source[:, :, first, :].reshape(wide, width),
                    source[:, :, second, :].reshape(wide, width),
                ],
                axis=1,
            )
            result = mm(matrix[...], both).astype(BF16)
            target[:, :, first, :] = result[:, :width].reshape(devices, 2, PATCH, width)
            target[:, :, second, :] = result[:, width:].reshape(devices, 2, PATCH, width)

    turn(x_ref, mid_ref, outer_ref)

    def step(q, carry):
        spectrum = mm(inner_ref[q], mid_ref[q].reshape(2 * rows, width)).reshape(2, rows, width)
        scale = scale_ref[q].astype(F32)
        back = spectrum * scale[None] - data_ref[:, q].astype(F32)
        wave = mm(inner_t_ref[q], back.astype(BF16).reshape(2 * rows, width))
        mid_ref[q] = wave.astype(BF16).reshape(2, rows, width)
        return carry

    lax.fori_loop(0, devices, step, 0, unroll=4)
    turn(mid_ref, out_ref, outer_t_ref)


def spectrum_inputs(gains, observed, vis_weight, devices):
    width = vis_weight.shape[0]

    def turned(value):
        shaped = value.astype(BF16).reshape(width, N // devices, devices)
        return shaped.transpose(2, 1, 0)

    gr, gi = gains[0], gains[1]
    scale = turned(vis_weight * (gr * gr + gi * gi))
    data = jnp.stack(
        [
            turned(vis_weight * (gr * observed[0] + gi * observed[1])),
            turned(vis_weight * (gr * observed[1] - gi * observed[0])),
        ]
    )
    return scale, data


def patch_gradient(state, scale, data):
    ty, tx = lax.axis_size("ty"), lax.axis_size("tx")
    devices = ty * tx
    rows, cols, _ = state.shape
    own = rows // tx
    slab = N // devices
    first, twist, second, second_t = (jnp.asarray(value) for value in row_constants())
    outer, outer_t, inner, inner_t = (
        jnp.asarray(value) for value in column_constants(devices, slab)
    )
    gathered = lax.all_to_all(
        state.reshape(tx, own, cols, PIXELS), "tx", split_axis=0, concat_axis=0, tiled=True
    )
    sent = pl.pallas_call(
        row_forward,
        out_shape=jax.ShapeDtypeStruct((PATCH, devices // PATCH, 2, slab, slab), BF16),
        compiler_params=PARAMS,
    )(gathered, first, twist, second)
    moved = lax.all_to_all(
        sent.reshape(devices, 2, slab, slab), ("ty", "tx"), split_axis=0, concat_axis=0, tiled=True
    )
    waves = pl.pallas_call(
        column_both,
        out_shape=jax.ShapeDtypeStruct((devices, 2, slab, slab), BF16),
        scratch_shapes=[pltpu.VMEM((devices, 2, slab, slab), BF16)],
        compiler_params=PARAMS,
    )(moved, scale, data, outer, outer_t, inner, inner_t)
    returned = lax.all_to_all(waves, ("ty", "tx"), split_axis=0, concat_axis=0, tiled=True)
    slabs = pl.pallas_call(
        row_inverse,
        out_shape=jax.ShapeDtypeStruct((tx, own, cols, PIXELS), BF16),
        compiler_params=PARAMS,
    )(returned.reshape(PATCH, devices // PATCH, 2, slab, slab), first, twist, second_t)
    grad = lax.all_to_all(slabs, "tx", split_axis=0, concat_axis=0, tiled=True)
    return grad.reshape(rows, cols, PIXELS)


def layer_norm(values, gain):
    centre = jnp.mean(values, axis=-1, keepdims=True)
    shifted = values - centre
    spread = jnp.mean(shifted * shifted, axis=-1, keepdims=True)
    return (shifted * lax.rsqrt(spread + EPSILON) * gain).astype(BF16)


def to_windows(band):
    rows, cols, feats = band.shape
    pieces = [
        band[:, w * WIN : (w + 1) * WIN, :].reshape(SPAN, feats) for w in range(cols // WIN)
    ]
    return jnp.concatenate(pieces, axis=0)


def from_windows(tokens, cols):
    feats = tokens.shape[-1]
    pieces = [
        tokens[w * SPAN : (w + 1) * SPAN].reshape(WIN, WIN, feats) for w in range(cols // WIN)
    ]
    return jnp.concatenate(pieces, axis=1)


def swin_band(flow, bias_ref, qkv_ref, proj_ref, up_ref, down_ref, gain_ref, mixed_ref, att_ref):
    tokens = flow.shape[0]
    normed = layer_norm(flow, gain_ref[0:1, :])
    depth = D // HEADS
    scale = 1.0 / math.sqrt(depth)
    mixed_ref[:, :D] = (mm(normed, qkv_ref[:, :D]) * scale).astype(BF16)
    mixed_ref[:, D:] = mm(normed, qkv_ref[:, D:]).astype(BF16)
    lane = lax.broadcasted_iota(jnp.int32, (SPAN, 2 * depth), 1)
    lower = lane < depth
    for w in range(tokens // SPAN):
        rows = slice(w * SPAN, (w + 1) * SPAN)
        bias = bias_ref[w]
        for p in range(HEADS // 2):
            lanes = slice(p * 2 * depth, (p + 1) * 2 * depth)
            query = mixed_ref[rows, lanes]
            key = mixed_ref[rows, D + p * 2 * depth : D + (p + 1) * 2 * depth]
            value = mixed_ref[rows, 2 * D + p * 2 * depth : 2 * D + (p + 1) * 2 * depth]
            zero = jnp.zeros_like(query)
            split = jnp.concatenate(
                [jnp.where(lower, query, zero), jnp.where(lower, zero, query)], axis=0
            )
            scores = mm(key, split, NT) + bias
            weights = jnp.exp(scores - jnp.max(scores, axis=0, keepdims=True))
            probs = weights * (1.0 / jnp.sum(weights, axis=0, keepdims=True))
            mixture = mm(probs.astype(BF16), value, TN)
            att_ref[rows, lanes] = jnp.where(lower, mixture[:SPAN], mixture[SPAN:]).astype(BF16)
    flow = flow + mm(att_ref[...], proj_ref[...])
    normed = layer_norm(flow, gain_ref[1:2, :])
    hidden_size = up_ref.shape[1]
    for c in range(hidden_size // D):
        part = slice(c * D, (c + 1) * D)
        hidden = jax.nn.gelu(mm(normed, up_ref[:, part]), approximate=True)
        flow = flow + mm(hidden.astype(BF16), down_ref[part, :])
    return flow


def first_kernel(
    zeta, state_ref, grad_ref, bias_ref, embed_ref, qkv_ref, proj_ref, up_ref, down_ref, gain_ref,
    half_ref, out_ref, mixed_ref, att_ref,
):
    half = state_ref[...] - zeta * grad_ref[...].astype(F32)
    half_ref[...] = half
    tokens = mm(to_windows(half).astype(BF16), embed_ref[...]).astype(BF16).astype(F32)
    flow = swin_band(
        tokens, bias_ref, qkv_ref, proj_ref, up_ref, down_ref, gain_ref, mixed_ref, att_ref
    )
    out_ref[...] = from_windows(flow, half.shape[1]).astype(BF16)


def second_kernel(
    shift_ref, grid_ref, bias_ref, qkv_ref, proj_ref, up_ref, down_ref, gain_ref, unembed_ref,
    out_ref, mixed_ref, att_ref,
):
    cols = out_ref.shape[1]
    top = pl.program_id(0) * WIN + shift_ref[0]
    wide = grid_ref[pl.ds(top, WIN)]
    place = lax.broadcasted_iota(jnp.int32, (cols, wide.shape[1]), 1)
    target = lax.broadcasted_iota(jnp.int32, (cols, wide.shape[1]), 0) + shift_ref[1]
    pick = jnp.where(place == target, 1.0, 0.0).astype(BF16)
    band = jnp.stack([mm(pick, wide[n]) for n in range(WIN)])
    flow = swin_band(
        to_windows(band), bias_ref, qkv_ref, proj_ref, up_ref, down_ref, gain_ref, mixed_ref, att_ref
    )
    estimate = mm(flow.astype(BF16), unembed_ref[...])
    out_ref[...] = from_windows(estimate, cols).astype(BF16)


def whole(array):
    zeros = (0,) * array.ndim
    return pl.BlockSpec(array.shape, lambda *_: zeros)


def band_spec(cols, feats):
    return pl.BlockSpec((WIN, cols, feats), lambda n, *_: (n, 0, 0))


def bias_spec(cols):
    return pl.BlockSpec((cols // WIN, SPAN, 2 * SPAN), lambda n, *_: (n, 0, 0))


def band_scratch(cols):
    return [pltpu.VMEM((WIN * cols, 3 * D), BF16), pltpu.VMEM((WIN * cols, D), BF16)]


def first_block(zeta, state, grad, bias, w_embed, weights):
    rows, cols, _ = state.shape
    return pl.pallas_call(
        functools.partial(first_kernel, zeta),
        grid=(rows // WIN,),
        in_specs=[band_spec(cols, PIXELS), band_spec(cols, PIXELS), bias_spec(cols), whole(w_embed)]
        + [whole(value) for value in weights],
        out_specs=[band_spec(cols, PIXELS), band_spec(cols, D)],
        out_shape=[
            jax.ShapeDtypeStruct((rows, cols, PIXELS), F32),
            jax.ShapeDtypeStruct((rows, cols, D), BF16),
        ],
        scratch_shapes=band_scratch(cols),
        compiler_params=PARAMS,
    )(state, grad, bias, w_embed, *weights)


def second_block(shift, grid, bias, w_unembed, weights, rows, cols):
    return pl.pallas_call(
        second_kernel,
        grid_spec=pltpu.PrefetchScalarGridSpec(
            num_scalar_prefetch=1,
            grid=(rows // WIN,),
            in_specs=[whole(grid), bias_spec(cols)]
            + [whole(value) for value in weights]
            + [whole(w_unembed)],
            out_specs=band_spec(cols, PIXELS),
            scratch_shapes=band_scratch(cols),
        ),
        out_shape=jax.ShapeDtypeStruct((rows, cols, PIXELS), BF16),
        compiler_params=PARAMS,
    )(shift, grid, bias, *weights, w_unembed)


def from_behind(shard, axis, by):
    size = lax.axis_size(axis)
    return lax.ppermute(shard, axis, [(i, (i + by) % size) for i in range(size)])


def with_next(grid):
    wide = jnp.concatenate([grid, from_behind(grid[:, :WIN], "tx", -1)], axis=1)
    return jnp.concatenate([wide, from_behind(wide[:WIN], "ty", -1)], axis=0)


def with_previous(grid):
    wide = jnp.concatenate([from_behind(grid[:, -WIN:], "tx", 1), grid], axis=1)
    return jnp.concatenate([from_behind(wide[-WIN:], "ty", 1), wide], axis=0)


def windows_of(grid):
    rows, cols = grid.shape
    shaped = grid.reshape(rows // WIN, WIN, cols // WIN, WIN).transpose(0, 2, 1, 3)
    return shaped.reshape(rows // WIN * (cols // WIN), SPAN)


def bias_of(labels, keep):
    allowed = jnp.ones((1, SPAN, SPAN), bool)
    if labels is not None:
        label = windows_of(labels)
        allowed = label[:, :, None] == label[:, None, :]
    if keep is not None:
        kept = windows_of(keep)[:, :, None] == 1
        allowed = allowed & (kept | jnp.eye(SPAN, dtype=bool)[None])
    bias = jnp.where(allowed, 0.0, -1e30).astype(F32)
    return jnp.concatenate([bias, bias], axis=2)


def region(index, shift):
    return jnp.where(index < TOK - WIN, 0, jnp.where(index < TOK - shift, 1, 2)).astype(jnp.int32)


def patches_of(picture):
    rows, cols = picture.shape
    shaped = picture.reshape(rows // PATCH, PATCH, cols // PATCH, PATCH).transpose(0, 2, 1, 3)
    return shaped.reshape(rows // PATCH, cols // PATCH, PIXELS)


def image_of(pieces):
    rows, cols = (pieces.shape[0], pieces.shape[1])
    shaped = pieces.reshape(rows, cols, PATCH, PATCH).transpose(0, 2, 1, 3)
    return shaped.reshape(rows * PATCH, cols * PATCH)


def per_device(
    image, noise, offsets, key_mask, gains, observed, vis_weight,
    w_embed, w_qkv, w_proj, w_up, w_down, w_unembed, norm_gains,
):
    rows = image.shape[0] // PATCH
    cols = image.shape[1] // PATCH
    devices = lax.axis_size("ty") * lax.axis_size("tx")
    fast = N // devices == TOK // 2
    row_index = lax.axis_index("ty") * rows + counting(rows)
    col_index = lax.axis_index("tx") * cols + counting(cols)
    weights = [
        (w_qkv[j], w_proj[j], w_up[j], w_down[j], norm_gains[j]) for j in range(w_qkv.shape[0])
    ]
    state = patches_of(image)
    if fast:
        scale, data = spectrum_inputs(gains, observed, vis_weight, devices)
    first_bias = bias_of(None, key_mask)
    for step in range(STEPS):
        if fast:
            grad = patch_gradient(state.astype(BF16), scale, data)
        else:
            grad = patches_of(plain_gradient(image_of(state), gains, observed, vis_weight))
        half, first = first_block(STEP_SIZES[step], state, grad, first_bias, w_embed, weights[0])
        shift_rows = offsets[step, 0]
        shift_cols = offsets[step, 1]
        labels = 3 * region(row_index, shift_rows)[:, None] + region(col_index, shift_cols)[None, :]
        second_bias = bias_of(labels, None)
        rolled = second_block(
            offsets[step], with_next(first), second_bias, w_unembed, weights[1], rows, cols
        )
        estimate = lax.dynamic_slice(
            with_previous(rolled),
            (WIN - shift_rows, WIN - shift_cols, jnp.zeros((), jnp.int32)),
            (rows, cols, PIXELS),
        )
        state = half - SIGMAS[step] * estimate.astype(F32)
        if step + 1 < STEPS:
            state = state + SIGMAS[step + 1] * patches_of(noise[step])
    return image_of(state) + SIGMAS[STEPS] * noise[STEPS - 1]


def solution(mesh):
    in_specs = (
        P("ty", "tx"),
        P(None, "ty", "tx"),
        P(),
        P("ty", "tx"),
        P(None, ("ty", "tx"), None),
        P(None, ("ty", "tx"), None),
        P(("ty", "tx"), None),
        P(),
        P(),
        P(),
        P(),
        P(),
        P(),
        P(),
    )
    out_specs = P("ty", "tx")
    return jax.shard_map(
        per_device, mesh=mesh, in_specs=in_specs, out_specs=out_specs, check_vma=False
    )
```

time: 1400 us -> 737 us (0.53)
  waiting for transfers between devices: 516 us -> 86.7 us
  matrix products: 296 us -> 0 us
  Pallas kernels: 0 us -> 288 us
  local copies, waits for them, and re-layouts: 383 us -> 131 us
  blocking collectives: 30.3 us -> 161 us
  other arithmetic: 100 us -> 31 us
  starting transfers between devices: 47.5 us -> 20.9 us
    ppermute x8, waiting for transfers between devices: 358 us -> 31.1 us  [from_behind(): lax.ppermute(shard, axis, [(i, (i + by) % size) for i in range(size)])]
    dot_general x84 -> x0, matrix products: 296 us -> none  [the longest x12 39.3 us: complex_einsum(): jnp.einsum(form, left[0], right[1], precision=HIGHEST)]
    pallas_call x0 -> x10, Pallas kernels: none -> 288 us  [the longest x2 116 us: second_block(): pl.pallas_call(second_kernel, grid_spec=pltpu.PrefetchScalarGridSpec(num_...]
    all_to_all x2 -> x5, blocking collectives: 30.3 us -> 161 us  [the longest x1 52.6 us: patch_gradient(): lax.all_to_all(sent.reshape(devices, 2, slab, slab), ('ty', 'tx'), split_...]
    another operation x12 -> x1, local copies, waits for them, and re-layouts: 105 us -> 0.81 us  [spectrum_inputs(): jnp.stack([turned(vis_weight * (gr * observed[0] + gi * observed[1])), tu...]
    all_to_all x10 -> x3, waiting for transfers between devices: 159 us -> 55.7 us  [the longest x1 36.1 us: patch_gradient(): lax.all_to_all(waves, ('ty', 'tx'), split_axis=0, concat_axis=0, tiled=True)]
    convert_element_type x28 -> x1, local copies, waits for them, and re-layouts: 81.7 us -> 0.83 us  [per_device(): grad = patch_gradient(state.astype(BF16), scale, data)]
    mul x10 -> x3, local copies, waits for them, and re-layouts: 67.2 us -> 23.4 us  [per_device(): state = state + SIGMAS[step + 1] * patches_of(noise[step])]
  transfers between devices with their start and end apart: 18 -> 11, of which waited for: 17 -> 10; matrix products, arithmetic and copies ran while one was open for 6% -> 12% of each run, Pallas kernels for 0% -> 0%
where the time goes in v1:
time: 737 us; the launch traced here: 727 us
  Pallas kernels  288 us (39%)
  blocking collectives  161 us (22%)
  local copies, waits for them, and re-layouts  131 us (18%)
  waiting for transfers between devices  86.7 us (12%)
  other arithmetic  31 us (4%)
  starting transfers between devices  20.9 us (3%)
  between operations  8.42 us (1%)
    pallas_call x2, Pallas kernels, second_block(): pl.pallas_call(second_kernel, grid_spec=pltpu.PrefetchScalarGridSpec(num_...  116 us
    pallas_call x2, Pallas kernels, first_block(): pl.pallas_call(functools.partial(first_kernel, zeta), grid=(rows // WIN,)...  109 us
    all_to_all x1, blocking collectives, patch_gradient(): lax.all_to_all(sent.reshape(devices, 2, slab, slab), ('ty', 'tx'), split_...  52.6 us
    all_to_all x1, blocking collectives, patch_gradient(): lax.all_to_all(waves, ('ty', 'tx'), split_axis=0, concat_axis=0, tiled=True)  52.4 us
    all_to_all x2, blocking collectives, patch_gradient(): lax.all_to_all(state.reshape(tx, own, cols, PIXELS), 'tx', split_axis=0,...  36.9 us
    all_to_all x1, waiting for transfers between devices, patch_gradient(): lax.all_to_all(waves, ('ty', 'tx'), split_axis=0, concat_axis=0, tiled=True)  36.1 us
    pallas_call x2, Pallas kernels, patch_gradient(): pl.pallas_call(column_both, out_shape=jax.ShapeDtypeStruct((devices, 2, s...  33.8 us
    ppermute x8, waiting for transfers between devices, from_behind(): lax.ppermute(shard, axis, [(i, (i + by) % size) for i in range(size)])  31.1 us
  transfers between devices with their start and end apart: 11, of which 10 were waited for; matrix products, arithmetic and copies ran while one was open for 12% of the time, Pallas kernels for 0%

profile of v1, /device:TPU:0, one launch (start us, length us, event | category | flops | bytes accessed | tf_op | source)
XLA Modules:
  0.0 727.3 jit_solution(12158617081280716909)
XLA Ops:
  0.0 10.4 %reshape.166 = f32[32,16,64,16]{3,2,1,0:T(8,128)} reshape(f32[512,1024]{1,0:T(8,128)} %param.22) | data formatting | bytes 4194304 | tf_op jit(solution)/shard_map/reshape | solution.py:483
  10.4 11.4 %copy.46 = f32[32,16,64,16]{2,3,1,0:T(8,128)} copy(f32[32,16,64,16]{3,2,1,0:T(8,128)} %reshape.166) | data formatting | bytes 4194304 | tf_op jit(solution)/shard_map/reshape | solution.py:483
  25.3 19.2 %all_to_all.40.x_ref = bf16[4,8,64,256]{3,2,1,0:T(8,128)(2,1)} all-to-all(bf16[4,8,64,256]{3,2,1,0:T(8,128)(2,1)S(1)} %copy.47), channel_id=1, replica_groups=mesh['ty'=8,'tx'=4] {'tx'}, dimensions={0} | all-to-all | bytes 2097152 | tf_op jit(solution)/shard_map/all_to_all | solution.py:276
  44.5 7.0 shard_map.208
  51.5 4.3 all-to-all-start.1
  58.7 4.7 fusion.15
  66.4 4.7 fusion.14
  79.9 5.1 fusion.1
  88.8 15.7 %all-to-all-done.1.x_ref = bf16[32,2,128,128]{3,2,1,0:T(8,128)(2,1)S(1)} async-done(((bf16[32,2,128,128]{3,2,1,0:T(8,128)(2,1)}), bf16[32,2,128,128]{3,2,1,0:T(8,128)(2,1)S(1)}, u32[]{:S(2)}, u32[]{:S(2)}) %all-to-all-start.1) | async-done | bytes 2097184 | tf_op jit(solution)/shard_map/all_to_all | solution.py:284
  105.9 16.9 %shard_map.209 = bf16[32,2,128,128]{3,2,1,0:T(8,128)(2,1)} custom-call(bf16[32,2,128,128]{3,2,1,0:T(8,128)(2,1)} %copy-done.2, bf16[32,128,128]{2,1,0:T(8,128)(2,1)} %bitcast.94, bf16[2,32,128,128]{3,2,1,0:T(8,128)(2,1)} %pad_maximum_fusion.2.data_ref, bf16[1024,1024]{1,0:T(8,128)(2,1)} %constant.84.clone.outer_ref, ...), custom_call_target="tpu_custom_call" | custom-call | tf_op jit(solution)/shard_map/pallas_call | solution.py:287
  122.8 4.4 all-to-all-start.2
  139.8 36.1 %all-to-all-done.2 = bf16[32,2,128,128]{3,2,1,0:T(8,128)(2,1)S(1)} async-done(((bf16[32,2,128,128]{3,2,1,0:T(8,128)(2,1)}), bf16[32,2,128,128]{3,2,1,0:T(8,128)(2,1)S(1)}, u32[]{:S(2)}, u32[]{:S(2)}) %all-to-all-start.2) | async-done | bytes 2097184 | tf_op jit(solution)/shard_map/all_to_all | solution.py:293
  177.2 7.9 %shard_map.210 = bf16[4,8,64,256]{3,2,1,0:T(8,128)(2,1)} custom-call(bf16[16,2,2,128,128]{4,3,2,1,0:T(8,128)(2,1)} %bitcast.97, bf16[256,512]{1,0:T(8,128)(2,1)} %constant.80.clone.first_ref, f32[2,256,256]{2,1,0:T(8,128)} %constant.81.clone.twist_ref, bf16[512,512]{1,0:T(8,128)(2,1)} %constant.83.clone.second_ref), custom_call_target="tpu_custom_call" | custom-call | tf_op jit(solution)/shard_map/pallas_call | solution.py:294
  194.4 4.4 slice_bitcast_fusion
  203.7 54.5 %shard_map.211 = (f32[32,64,256]{2,1,0:T(8,128)}, bf16[32,64,512]{2,1,0:T(8,128)(2,1)}) custom-call(f32[32,64,256]{2,1,0:T(8,128)} %copy.59.state_ref, bf16[32,64,256]{2,1,0:T(8,128)(2,1)} %bitcast.101, f32[32,64,128]{2,1,0:T(8,128)} %pad_maximum_fusion.3.bias_ref, bf16[256,512]{1,0:T(8,128)(2,1)} %embed_ref.3, bf16[512,1536]{1,0:T(8,128)(2,1)} %get-tuple-element.27.qkv_ref, ...), custom_call_target="tpu_custom_call" | custom-call | tf_op jit(solution)/shard_map/pallas_call | solution.py:412
  269.3 5.2 collective-permute-done.1
  276.3 58.1 %shard_map.212 = bf16[32,64,256]{2,1,0:T(8,128)(2,1)} custom-call(s32[2]{0:T(128)} %get-tuple-element.33.shift_ref, bf16[40,72,512]{2,1,0:T(8,128)(2,1)} %pad_maximum_fusion.grid_ref, f32[32,64,128]{2,1,0:T(8,128)} %pad_maximum_fusion.4.bias_ref, bf16[512,1536]{1,0:T(8,128)(2,1)} %get-tuple-element.26.qkv_ref, bf16[512,512]{1,0:T(8,128)(2,1)} %get-tuple-element.28.proj_ref, ...), custom_call_target="tpu_custom_call" | custom-call | tf_op jit(solution)/shard_map/pallas_call | solution.py:428
  344.6 9.1 %mul.100 = f32[32,16,64,16]{3,2,1,0:T(8,128)} reshape(f32[1,512,1024]{2,1,0:T(8,128)S(1)} %slice_multiply_fusion) | data formatting | bytes 4194304 | tf_op jit(solution)/shard_map/mul | solution.py:530
  353.6 11.4 %copy.60 = f32[32,64,16,16]{1,3,2,0:T(8,128)} copy(f32[32,64,16,16]{3,1,2,0:T(8,128)} %bitcast.90) | data formatting | bytes 4194304 | tf_op jit(solution)/shard_map/mul | solution.py:530
  373.1 17.7 %all_to_all.41.x_ref = bf16[4,8,64,256]{3,2,1,0:T(8,128)(2,1)} all-to-all(bf16[4,8,64,256]{3,2,1,0:T(8,128)(2,1)S(1)} %bitcast.103), channel_id=1, replica_groups=mesh['ty'=8,'tx'=4] {'tx'}, dimensions={0} | all-to-all | bytes 2097152 | tf_op jit(solution)/shard_map/all_to_all | solution.py:276
  390.9 7.0 shard_map.213
  397.9 52.6 %all_to_all.42.x_ref = bf16[32,2,128,128]{3,2,1,0:T(8,128)(2,1)} all-to-all(bf16[32,2,128,128]{3,2,1,0:T(8,128)(2,1)} %bitcast.100), channel_id=1, replica_groups=mesh['ty'=8,'tx'=4] {'ty','tx'}, dimensions={0} | all-to-all | bytes 4194304 | tf_op jit(solution)/shard_map/all_to_all | solution.py:284
  450.5 16.9 %shard_map.214 = bf16[32,2,128,128]{3,2,1,0:T(8,128)(2,1)} custom-call(bf16[32,2,128,128]{3,2,1,0:T(8,128)(2,1)} %all_to_all.42.x_ref, bf16[32,128,128]{2,1,0:T(8,128)(2,1)} %bitcast.95, bf16[2,32,128,128]{3,2,1,0:T(8,128)(2,1)} %pad_maximum_fusion.2.data_ref, bf16[1024,1024]{1,0:T(8,128)(2,1)} %constant.84.clone.outer_ref, ...), custom_call_target="tpu_custom_call" | custom-call | tf_op jit(solution)/shard_map/pallas_call | solution.py:287
  467.4 52.4 %all_to_all.43 = bf16[32,2,128,128]{3,2,1,0:T(8,128)(2,1)} all-to-all(bf16[32,2,128,128]{3,2,1,0:T(8,128)(2,1)} %shard_map.214), channel_id=1, replica_groups=mesh['ty'=8,'tx'=4] {'ty','tx'}, dimensions={0} | all-to-all | bytes 4194304 | tf_op jit(solution)/shard_map/all_to_all | solution.py:293
  519.8 7.9 %shard_map.215 = bf16[4,8,64,256]{3,2,1,0:T(8,128)(2,1)} custom-call(bf16[16,2,2,128,128]{4,3,2,1,0:T(8,128)(2,1)} %bitcast.99, bf16[256,512]{1,0:T(8,128)(2,1)} %constant.80.clone.first_ref, f32[2,256,256]{2,1,0:T(8,128)} %constant.81.clone.twist_ref, bf16[512,512]{1,0:T(8,128)(2,1)} %constant.83.clone.second_ref), custom_call_target="tpu_custom_call" | custom-call | tf_op jit(solution)/shard_map/pallas_call | solution.py:294
  527.7 18.8 %all_to_all.44 = bf16[4,8,64,256]{3,2,1,0:T(8,128)(2,1)} all-to-all(bf16[4,8,64,256]{3,2,1,0:T(8,128)(2,1)} %shard_map.215), channel_id=1, replica_groups=mesh['ty'=8,'tx'=4] {'tx'}, dimensions={0} | all-to-all | bytes 2097152 | tf_op jit(solution)/shard_map/all_to_all | solution.py:299
  546.5 54.5 %shard_map.216 = (f32[32,64,256]{2,1,0:T(8,128)}, bf16[32,64,512]{2,1,0:T(8,128)(2,1)}) custom-call(f32[32,64,256]{2,1,0:T(8,128)} %get-tuple-element.14.state_ref, bf16[32,64,256]{2,1,0:T(8,128)(2,1)} %bitcast.102, f32[32,64,128]{2,1,0:T(8,128)} %pad_maximum_fusion.3.bias_ref, bf16[256,512]{1,0:T(8,128)(2,1)} %embed_ref.3, ...), custom_call_target="tpu_custom_call" | custom-call | tf_op jit(solution)/shard_map/pallas_call | solution.py:412
  618.2 57.5 %shard_map.217 = bf16[32,64,256]{2,1,0:T(8,128)(2,1)} custom-call(s32[2]{0:T(128)} %get-tuple-element.32.shift_ref, bf16[40,72,512]{2,1,0:T(8,128)(2,1)} %pad_maximum_fusion.1.grid_ref, f32[32,64,128]{2,1,0:T(8,128)} %pad_maximum_fusion.5.bias_ref, bf16[512,1536]{1,0:T(8,128)(2,1)} %get-tuple-element.26.qkv_ref, ...), custom_call_target="tpu_custom_call" | custom-call | tf_op jit(solution)/shard_map/pallas_call | solution.py:428
  679.3 4.8 collective-permute-done.6
  687.7 5.3 collective-permute-done.7
  698.8 10.5 %copy.63 = f32[32,16,64,16]{3,2,1,0:T(8,128)} copy(f32[32,16,64,16]{2,3,1,0:T(8,128)} %bitcast.93) | data formatting | bytes 4194304 | tf_op jit(solution)/shard_map/transpose | solution.py:489
  709.4 14.2 %reshape.179 = f32[512,1024]{1,0:T(8,128)S(1)} reshape(f32[32,16,64,16]{3,2,1,0:T(8,128)} %copy.63) | data formatting | bytes 4194304 | tf_op jit(solution)/shard_map/reshape | solution.py:490
  (93 shorter events, 108.3 us)
Async XLA Ops:
  51.5 53.0 %all-to-all-start.1 = ((bf16[32,2,128,128]{3,2,1,0:T(8,128)(2,1)}), bf16[32,2,128,128]{3,2,1,0:T(8,128)(2,1)S(1)}, u32[]{:S(2)}, u32[]{:S(2)}) async-start(bf16[32,2,128,128]{3,2,1,0:T(8,128)(2,1)} %bitcast.98), calls=%async_computation.1 | async-start | bytes 4194304 | tf_op jit(solution)/shard_map/all_to_all | solution.py:284
  104.5 1.3 copy-start.2
  122.8 4.4 copy-start.9
  122.8 4.7 copy-start.10
  122.8 8.0 %copy-start.11 = (f32[2,2,512]{2,1,0:T(2,128)S(1)}, f32[2,2,512]{2,1,0:T(2,128)}, u32[]{:S(2)}) copy-start(f32[2,2,512]{2,1,0:T(2,128)} %param.35) | copy-start | bytes 24580
  122.8 53.1 %all-to-all-start.2 = ((bf16[32,2,128,128]{3,2,1,0:T(8,128)(2,1)}), bf16[32,2,128,128]{3,2,1,0:T(8,128)(2,1)S(1)}, u32[]{:S(2)}, u32[]{:S(2)}) async-start(bf16[32,2,128,128]{3,2,1,0:T(8,128)(2,1)} %shard_map.209), calls=%async_computation.2 | async-start | bytes 4194304 | tf_op jit(solution)/shard_map/all_to_all | solution.py:293
  130.7 3.2 copy-start.7
  133.9 3.3 copy-start.6
  175.9 1.3 copy-start.3
  185.1 17.7 %all-to-all-start.3 = ((bf16[4,8,64,256]{3,2,1,0:T(8,128)(2,1)}), bf16[4,8,64,256]{3,2,1,0:T(8,128)(2,1)S(1)}, u32[]{:S(2)}, u32[]{:S(2)}) async-start(bf16[4,8,64,256]{3,2,1,0:T(8,128)(2,1)} %shard_map.210), calls=%async_computation.3 | async-start | bytes 2097152 | tf_op jit(solution)/shard_map/all_to_all | solution.py:299
  202.7 1.0 copy-start.5
  259.2 7.3 %collective-permute-start = (bf16[32,8,512]{2,1,0:T(8,128)(2,1)S(1)}, bf16[32,8,512]{2,1,0:T(8,128)(2,1)S(1)}, u32[]{:S(2)}, u32[]{:S(2)}) collective-permute-start(bf16[32,8,512]{2,1,0:T(8,128)(2,1)S(1)} %slice.102), channel_id=1, source_target_pairs={{0,3},{1,0},{2,1},{3,2},{4,7},{5,4},{6,5},{7,6},{8,11},{9,8},{10,9... | collective-permute-start | bytes 786440 | tf_op jit(solution)/shard_map/ppermute | solution.py:446
  266.5 7.9 %collective-permute-start.1 = (bf16[8,72,512]{2,1,0:T(8,128)(2,1)S(1)}, bf16[8,72,512]{2,1,0:T(8,128)(2,1)S(1)}, u32[]{:S(2)}, u32[]{:S(2)}) collective-permute-start(bf16[8,72,512]{2,1,0:T(8,128)(2,1)S(1)} %slice.122), channel_id=1, source_target_pairs={{0,28},{4,0},{8,4},{12,8},{16,12},{20,16},{24,20},{28,24},{1,29},{... | collective-permute-start | bytes 1769480 | tf_op jit(solution)/shard_map/ppermute | solution.py:446
  276.3 68.1 %copy-start.4 = (f32[2,512,1024]{2,1,0:T(8,128)S(1)}, f32[2,512,1024]{2,1,0:T(8,128)}, u32[]{:S(2)}) copy-start(f32[2,512,1024]{2,1,0:T(8,128)} %param.23) | copy-start | bytes 12582916
  335.3 7.3 %collective-permute-start.2 = (bf16[32,8,256]{2,1,0:T(8,128)(2,1)S(1)}, bf16[32,8,256]{2,1,0:T(8,128)(2,1)S(1)}, u32[]{:S(2)}, u32[]{:S(2)}) collective-permute-start(bf16[32,8,256]{2,1,0:T(8,128)(2,1)S(1)} %slice.123), channel_id=1, source_target_pairs={{0,1},{1,2},{2,3},{3,0},{4,5},{5,6},{6,7},{7,4},{8,9},{9,10},{10,1... | collective-permute-start | bytes 393224 | tf_op jit(solution)/shard_map/ppermute | solution.py:446
  344.3 25.0 %collective-permute-start.3 = (bf16[8,72,256]{2,1,0:T(8,128)(2,1)}, bf16[8,72,256]{2,1,0:T(8,128)(2,1)}, u32[]{:S(2)}, u32[]{:S(2)}) collective-permute-start(bf16[8,72,256]{2,1,0:T(8,128)(2,1)} %pad_maximum_fusion.7), channel_id=1, source_target_pairs={{0,4},{4,8},{8,12},{12,16},{16,20},{20,24},{24,28},{28,0},{1,5},{5... | collective-permute-start | bytes 884744 | tf_op jit(solution)/shard_map/ppermute | solution.py:446
  365.1 4.2 copy-start
  601.9 6.7 collective-permute-start.4
  608.7 7.7 %collective-permute-start.5 = (bf16[8,72,512]{2,1,0:T(8,128)(2,1)S(1)}, bf16[8,72,512]{2,1,0:T(8,128)(2,1)S(1)}, u32[]{:S(2)}, u32[]{:S(2)}) collective-permute-start(bf16[8,72,512]{2,1,0:T(8,128)(2,1)S(1)} %slice.124), channel_id=1, source_target_pairs={{0,28},{4,0},{8,4},{12,8},{16,12},{20,16},{24,20},{28,24},{1,29},{... | collective-permute-start | bytes 1769480 | tf_op jit(solution)/shard_map/ppermute | solution.py:446
  675.8 18.0 %copy-start.1 = (bf16[32,64,256]{2,1,0:T(8,128)(2,1)S(1)}, bf16[32,64,256]{2,1,0:T(8,128)(2,1)}, u32[]{:S(2)}) copy-start(bf16[32,64,256]{2,1,0:T(8,128)(2,1)} %shard_map.217) | copy-start | bytes 3145732
  676.8 7.3 %collective-permute-start.6 = (bf16[32,8,256]{2,1,0:T(8,128)(2,1)S(1)}, bf16[32,8,256]{2,1,0:T(8,128)(2,1)S(1)}, u32[]{:S(2)}, u32[]{:S(2)}) collective-permute-start(bf16[32,8,256]{2,1,0:T(8,128)(2,1)S(1)} %slice.125), channel_id=1, source_target_pairs={{0,1},{1,2},{2,3},{3,0},{4,5},{5,6},{6,7},{7,4},{8,9},{9,10},{10,1... | collective-permute-start | bytes 393224 | tf_op jit(solution)/shard_map/ppermute | solution.py:446
  685.1 8.0 %collective-permute-start.7 = (bf16[8,72,256]{2,1,0:T(8,128)(2,1)S(1)}, bf16[8,72,256]{2,1,0:T(8,128)(2,1)S(1)}, u32[]{:S(2)}, u32[]{:S(2)}) collective-permute-start(bf16[8,72,256]{2,1,0:T(8,128)(2,1)S(1)} %pad_maximum_fusion.6), channel_id=1, source_target_pairs={{0,4},{4,8},{8,12},{12,16},{16,20},{20,24},{24,28},{28,0},{1,5},{5... | collective-permute-start | bytes 884744 | tf_op jit(solution)/shard_map/ppermute | solution.py:446
  693.1 0.7 copy-start.8

commit v2 on v1

--- a/solution.py
+++ b/solution.py
@@ -18,6 +18,7 @@
 HEADS = 8
 STEPS = 2
 SPAN = WIN * WIN
+LANES = 128
 TOK = N // PATCH
 
 SIGMAS = (0.8, 0.5, 0.3)
@@ -26,6 +27,8 @@
 HIGHEST = lax.Precision.HIGHEST
 BF16 = jnp.bfloat16
 F32 = jnp.float32
+GELU_IN = math.sqrt(2.0 / math.pi)
+GELU_CUBE = 0.044715 * GELU_IN
 VMEM_LIMIT = 56 * 1024 * 1024
 PARAMS = pltpu.CompilerParams(vmem_limit_bytes=VMEM_LIMIT)
 TN = (((0,), (0,)), ((), ()))
@@ -135,12 +138,12 @@
     k = np.arange(TOK)
     angle = wheel(TOK, k[:, None] * k[None, :])
     first = np.concatenate([np.cos(angle), -np.sin(angle)], axis=1)
-    b = np.tile(np.arange(PATCH), PATCH)
+    b = np.repeat(np.arange(PATCH), PATCH)
     angle = wheel(N, b[:, None] * k[None, :])
     twist = np.stack([np.cos(angle), -np.sin(angle)])
     p = np.arange(PATCH)
     small = embed_complex(wheel(PATCH, p[:, None] * p[None, :]), 1, 1)
-    second = np.einsum("kpqb,xy->kpxqyb", small, np.eye(PATCH)).reshape(2 * PIXELS, 2 * PIXELS)
+    second = np.einsum("kpqb,xy->kpxqby", small, np.eye(PATCH)).reshape(2 * PIXELS, 2 * PIXELS)
     return (
         first.astype(ml_dtypes.bfloat16),
         twist.astype(np.float32),
@@ -323,58 +326,76 @@
     return jnp.concatenate(pieces, axis=1)
 
 
-def swin_band(flow, bias_ref, qkv_ref, proj_ref, up_ref, down_ref, gain_ref, mixed_ref, att_ref):
-    tokens = flow.shape[0]
+def swin_band(
+    flow, bias_ref, qkv_ref, proj_ref, up_ref, down_ref, gain_ref, mixed_ref, score_ref, prob_ref
+):
+    count = flow.shape[0] // SPAN
+    pairs = HEADS // 2
+    depth = D // HEADS
+    wide = 2 * depth
     normed = layer_norm(flow, gain_ref[0:1, :])
-    depth = D // HEADS
     scale = 1.0 / math.sqrt(depth)
     mixed_ref[:, :D] = (mm(normed, qkv_ref[:, :D]) * scale).astype(BF16)
-    mixed_ref[:, D:] = mm(normed, qkv_ref[:, D:]).astype(BF16)
-    lane = lax.broadcasted_iota(jnp.int32, (SPAN, 2 * depth), 1)
-    lower = lane < depth
-    for w in range(tokens // SPAN):
+    mixed_ref[:, D : 2 * D] = mm(normed, qkv_ref[:, D : 2 * D]).astype(BF16)
+    mixed_ref[:, 2 * D :] = mm(normed, qkv_ref[:, 2 * D :]).astype(BF16)
+    lower = lax.broadcasted_iota(jnp.int32, (SPAN, wide), 1) < depth
+    for w in range(count):
         rows = slice(w * SPAN, (w + 1) * SPAN)
-        bias = bias_ref[w]
-        for p in range(HEADS // 2):
-            lanes = slice(p * 2 * depth, (p + 1) * 2 * depth)
-            query = mixed_ref[rows, lanes]
-            key = mixed_ref[rows, D + p * 2 * depth : D + (p + 1) * 2 * depth]
-            value = mixed_ref[rows, 2 * D + p * 2 * depth : 2 * D + (p + 1) * 2 * depth]
+        for p in range(pairs):
+            query = mixed_ref[rows, p * wide : (p + 1) * wide]
+            key = mixed_ref[rows, D + p * wide : D + (p + 1) * wide]
             zero = jnp.zeros_like(query)
             split = jnp.concatenate(
                 [jnp.where(lower, query, zero), jnp.where(lower, zero, query)], axis=0
             )
-            scores = mm(key, split, NT) + bias
+            score_ref[w, :, p * wide : (p + 1) * wide] = mm(key, split, NT)
+    for w in range(count):
+        bias = bias_ref[w]
+        for p in range(pairs):
+            lanes = slice(p * wide, (p + 1) * wide)
+            scores = score_ref[w, :, lanes] + bias
             weights = jnp.exp(scores - jnp.max(scores, axis=0, keepdims=True))
-            probs = weights * (1.0 / jnp.sum(weights, axis=0, keepdims=True))
-            mixture = mm(probs.astype(BF16), value, TN)
-            att_ref[rows, lanes] = jnp.where(lower, mixture[:SPAN], mixture[SPAN:]).astype(BF16)
-    flow = flow + mm(att_ref[...], proj_ref[...])
+            share = 1.0 / jnp.sum(weights, axis=0, keepdims=True)
+            prob_ref[w, :, lanes] = (weights * share).astype(BF16)
+    for w in range(count):
+        rows = slice(w * SPAN, (w + 1) * SPAN)
+        for p in range(pairs):
+            lanes = slice(p * wide, (p + 1) * wide)
+            value = mixed_ref[rows, 2 * D + p * wide : 2 * D + (p + 1) * wide]
+            mixture = mm(prob_ref[w, :, lanes], value, TN)
+            mixed_ref[rows, lanes] = jnp.where(lower, mixture[:SPAN], mixture[SPAN:]).astype(BF16)
+    flow = flow + mm(mixed_ref[:, :D], proj_ref[...])
     normed = layer_norm(flow, gain_ref[1:2, :])
-    hidden_size = up_ref.shape[1]
-    for c in range(hidden_size // D):
-        part = slice(c * D, (c + 1) * D)
-        hidden = jax.nn.gelu(mm(normed, up_ref[:, part]), approximate=True)
-        flow = flow + mm(hidden.astype(BF16), down_ref[part, :])
-    return flow
+    chunks = up_ref.shape[1] // D
+    total = jnp.zeros_like(flow)
+    ahead = mm(normed, up_ref[:, :D])
+    for c in range(chunks):
+        value = ahead
+        if c + 1 < chunks:
+            ahead = mm(normed, up_ref[:, (c + 1) * D : (c + 2) * D])
+        inside = value * (GELU_IN + GELU_CUBE * (value * value))
+        active = (value + value * jnp.tanh(inside)).astype(BF16)
+        total = total + mm(active, down_ref[c * D : (c + 1) * D, :])
+    return flow + 0.5 * total
 
 
 def first_kernel(
     zeta, state_ref, grad_ref, bias_ref, embed_ref, qkv_ref, proj_ref, up_ref, down_ref, gain_ref,
-    half_ref, out_ref, mixed_ref, att_ref,
+    half_ref, out_ref, mixed_ref, score_ref, prob_ref,
 ):
     half = state_ref[...] - zeta * grad_ref[...].astype(F32)
     half_ref[...] = half
     tokens = mm(to_windows(half).astype(BF16), embed_ref[...]).astype(BF16).astype(F32)
     flow = swin_band(
-        tokens, bias_ref, qkv_ref, proj_ref, up_ref, down_ref, gain_ref, mixed_ref, att_ref
+        tokens, bias_ref, qkv_ref, proj_ref, up_ref, down_ref, gain_ref, mixed_ref, score_ref,
+        prob_ref,
     )
     out_ref[...] = from_windows(flow, half.shape[1]).astype(BF16)
 
 
 def second_kernel(
     shift_ref, grid_ref, bias_ref, qkv_ref, proj_ref, up_ref, down_ref, gain_ref, unembed_ref,
-    out_ref, mixed_ref, att_ref,
+    out_ref, mixed_ref, score_ref, prob_ref,
 ):
     cols = out_ref.shape[1]
     top = pl.program_id(0) * WIN + shift_ref[0]
@@ -384,7 +405,8 @@
     pick = jnp.where(place == target, 1.0, 0.0).astype(BF16)
     band = jnp.stack([mm(pick, wide[n]) for n in range(WIN)])
     flow = swin_band(
-        to_windows(band), bias_ref, qkv_ref, proj_ref, up_ref, down_ref, gain_ref, mixed_ref, att_ref
+        to_windows(band), bias_ref, qkv_ref, proj_ref, up_ref, down_ref, gain_ref, mixed_ref,
+        score_ref, prob_ref,
     )
     estimate = mm(flow.astype(BF16), unembed_ref[...])
     out_ref[...] = from_windows(estimate, cols).astype(BF16)
@@ -395,6 +417,11 @@
     return pl.BlockSpec(array.shape, lambda *_: zeros)
 
 
+def member(array, j):
+    place = (j,) + (0,) * (array.ndim - 1)
+    return pl.BlockSpec((None,) + array.shape[1:], lambda *_: place)
+
+
 def band_spec(cols, feats):
     return pl.BlockSpec((WIN, cols, feats), lambda n, *_: (n, 0, 0))
 
@@ -404,7 +431,12 @@
 
 
 def band_scratch(cols):
-    return [pltpu.VMEM((WIN * cols, 3 * D), BF16), pltpu.VMEM((WIN * cols, D), BF16)]
+    count = cols // WIN
+    return [
+        pltpu.VMEM((WIN * cols, 3 * D), BF16),
+        pltpu.VMEM((count, SPAN, HEADS * SPAN), F32),
+        pltpu.VMEM((count, SPAN, HEADS * SPAN), BF16),
+    ]
 
 
 def first_block(zeta, state, grad, bias, w_embed, weights):
@@ -413,7 +445,7 @@
         functools.partial(first_kernel, zeta),
         grid=(rows // WIN,),
         in_specs=[band_spec(cols, PIXELS), band_spec(cols, PIXELS), bias_spec(cols), whole(w_embed)]
-        + [whole(value) for value in weights],
+        + [member(value, 0) for value in weights],
         out_specs=[band_spec(cols, PIXELS), band_spec(cols, D)],
         out_shape=[
             jax.ShapeDtypeStruct((rows, cols, PIXELS), F32),
@@ -431,7 +463,7 @@
             num_scalar_prefetch=1,
             grid=(rows // WIN,),
             in_specs=[whole(grid), bias_spec(cols)]
-            + [whole(value) for value in weights]
+            + [member(value, 1) for value in weights]
             + [whole(w_unembed)],
             out_specs=band_spec(cols, PIXELS),
             scratch_shapes=band_scratch(cols),
@@ -478,16 +510,94 @@
     return jnp.where(index < TOK - WIN, 0, jnp.where(index < TOK - shift, 1, 2)).astype(jnp.int32)
 
 
-def patches_of(picture):
-    rows, cols = picture.shape
-    shaped = picture.reshape(rows // PATCH, PATCH, cols // PATCH, PATCH).transpose(0, 2, 1, 3)
-    return shaped.reshape(rows // PATCH, cols // PATCH, PIXELS)
-
-
-def image_of(pieces):
-    rows, cols = (pieces.shape[0], pieces.shape[1])
-    shaped = pieces.reshape(rows, cols, PATCH, PATCH).transpose(0, 2, 1, 3)
-    return shaped.reshape(rows * PATCH, cols * PATCH)
+@functools.lru_cache(maxsize=None)
+def lane_order(cols):
+    parts = LANES // cols
+    groups = PATCH // parts
+    lane = np.arange(PATCH * cols)
+    g, h, k = lane // LANES, lane % LANES // cols, lane % cols
+    source = PATCH * k + h * groups + g
+    matrix = np.zeros((PATCH * cols, PATCH * cols), np.float32)
+    matrix[source, lane] = 1.0
+    return matrix.astype(ml_dtypes.bfloat16), np.ascontiguousarray(matrix.T).astype(
+        ml_dtypes.bfloat16
+    )
+
+
+def move_lanes(values, matrix):
+    high = values.astype(BF16)
+    low = (values - high.astype(F32)).astype(BF16)
+    return mm(high, matrix) + mm(low, matrix)
+
+
+def to_patches_kernel(tile_ref, order_ref, out_ref):
+    count, cols, _ = out_ref.shape
+    parts = LANES // cols
+    groups = PATCH // parts
+    ordered = move_lanes(tile_ref[...], order_ref[...])
+    for i in range(count):
+        band = ordered[i * PATCH : (i + 1) * PATCH]
+        stacked = jnp.concatenate(
+            [band[:, g * LANES : (g + 1) * LANES] for g in range(groups)], axis=0
+        )
+        turned = stacked.T
+        out_ref[i] = jnp.concatenate(
+            [turned[h * cols : (h + 1) * cols] for h in range(parts)], axis=1
+        )
+
+
+def to_tile_kernel(scale, patch_ref, noise_ref, order_ref, out_ref):
+    count, cols, _ = patch_ref.shape
+    parts = LANES // cols
+    groups = PATCH // parts
+    width = groups * PATCH
+    bands = []
+    for i in range(count):
+        patch = patch_ref[i]
+        stacked = jnp.concatenate(
+            [patch[:, h * width : (h + 1) * width] for h in range(parts)], axis=0
+        )
+        turned = stacked.T
+        bands.append(
+            jnp.concatenate([turned[g * PATCH : (g + 1) * PATCH] for g in range(groups)], axis=1)
+        )
+    moved = move_lanes(jnp.concatenate(bands, axis=0), order_ref[...])
+    out_ref[...] = moved + scale * noise_ref[...]
+
+
+def patches_of(tiles, j):
+    rows, cols = tiles.shape[1] // PATCH, tiles.shape[2] // PATCH
+    order = jnp.asarray(lane_order(cols)[0])
+    step = rows // 4
+    return pl.pallas_call(
+        to_patches_kernel,
+        grid=(rows // step,),
+        in_specs=[
+            pl.BlockSpec((None, step * PATCH, cols * PATCH), lambda n: (j, n, 0)),
+            whole(order),
+        ],
+        out_specs=pl.BlockSpec((step, cols, PIXELS), lambda n: (n, 0, 0)),
+        out_shape=jax.ShapeDtypeStruct((rows, cols, PIXELS), F32),
+        compiler_params=PARAMS,
+    )(tiles, order)
+
+
+def tile_of(patches, scale, noise, j):
+    rows, cols, _ = patches.shape
+    order = jnp.asarray(lane_order(cols)[1])
+    step = rows // 4
+    return pl.pallas_call(
+        functools.partial(to_tile_kernel, scale),
+        grid=(rows // step,),
+        in_specs=[
+            pl.BlockSpec((step, cols, PIXELS), lambda n: (n, 0, 0)),
+            pl.BlockSpec((None, step * PATCH, cols * PATCH), lambda n: (j, n, 0)),
+            whole(order),
+        ],
+        out_specs=pl.BlockSpec((step * PATCH, cols * PATCH), lambda n: (n, 0)),
+        out_shape=jax.ShapeDtypeStruct((rows * PATCH, cols * PATCH), F32),
+        compiler_params=PARAMS,
+    )(patches, noise, order)
 
 
 def per_device(
@@ -500,10 +610,10 @@
     fast = N // devices == TOK // 2
     row_index = lax.axis_index("ty") * rows + counting(rows)
     col_index = lax.axis_index("tx") * cols + counting(cols)
-    weights = [
-        (w_qkv[j], w_proj[j], w_up[j], w_down[j], norm_gains[j]) for j in range(w_qkv.shape[0])
-    ]
-    state = patches_of(image)
+    weights = (w_qkv, w_proj, w_up, w_down, norm_gains)
+    w_embed = w_embed.reshape(PATCH, PATCH, D).transpose(1, 0, 2).reshape(PIXELS, D)
+    w_unembed = w_unembed.reshape(D, PATCH, PATCH).transpose(0, 2, 1).reshape(D, PIXELS)
+    state = patches_of(image[None], 0)
     if fast:
         scale, data = spectrum_inputs(gains, observed, vis_weight, devices)
     first_bias = bias_of(None, key_mask)
@@ -511,14 +621,15 @@
         if fast:
             grad = patch_gradient(state.astype(BF16), scale, data)
         else:
-            grad = patches_of(plain_gradient(image_of(state), gains, observed, vis_weight))
-        half, first = first_block(STEP_SIZES[step], state, grad, first_bias, w_embed, weights[0])
+            grad = plain_gradient(tile_of(state, 0.0, noise, 0), gains, observed, vis_weight)
+            grad = patches_of(grad.astype(F32)[None], 0).astype(BF16)
+        half, first = first_block(STEP_SIZES[step], state, grad, first_bias, w_embed, weights)
         shift_rows = offsets[step, 0]
         shift_cols = offsets[step, 1]
         labels = 3 * region(row_index, shift_rows)[:, None] + region(col_index, shift_cols)[None, :]
         second_bias = bias_of(labels, None)
         rolled = second_block(
-            offsets[step], with_next(first), second_bias, w_unembed, weights[1], rows, cols
+            offsets[step], with_next(first), second_bias, w_unembed, weights, rows, cols
         )
         estimate = lax.dynamic_slice(
             with_previous(rolled),
@@ -527,8 +638,8 @@
         )
         state = half - SIGMAS[step] * estimate.astype(F32)
         if step + 1 < STEPS:
-            state = state + SIGMAS[step + 1] * patches_of(noise[step])
-    return image_of(state) + SIGMAS[STEPS] * noise[STEPS - 1]
+            state = state + SIGMAS[step + 1] * patches_of(noise, step)
+    return tile_of(state, SIGMAS[STEPS], noise, STEPS - 1)
 
 
 def solution(mesh):

time: 737 us -> 564 us (0.77)
  Pallas kernels: 288 us -> 192 us
  local copies, waits for them, and re-layouts: 131 us -> 40.7 us
  waiting for transfers between devices: 86.7 us -> 105 us
    pallas_call x2, Pallas kernels: 116 us -> 56.8 us  [second_block(): pl.pallas_call(second_kernel, grid_spec=pltpu.PrefetchScalarGridSpec(num_...]
    pallas_call x2, Pallas kernels: 109 us -> 51.8 us  [first_block(): pl.pallas_call(functools.partial(first_kernel, zeta), grid=(rows // WIN,)...]
    reshape x4 -> x2, local copies, waits for them, and re-layouts: 39.8 us -> 1.69 us  [the longest x1 0.85 us: per_device(): w_embed.reshape(PATCH, PATCH, D).transpose(1, 0, 2).reshape(PIXELS, D)]
    mul x3 -> x0, local copies, waits for them, and re-layouts: 23.4 us -> none  [per_device(): state = state + SIGMAS[step + 1] * patches_of(noise[step])]
    pallas_call x0 -> x3, Pallas kernels: none -> 20 us  [the longest x2 13.1 us: patches_of(): pl.pallas_call(to_patches_kernel, grid=(rows // step,), in_specs=[pl.Bloc...]
    squeeze x5 -> x0, local copies, waits for them, and re-layouts: 11.7 us -> none  [the longest x1 4.43 us: per_device(): w_down[j]]
    all_to_all x1, waiting for transfers between devices: 36.1 us -> 47.6 us  [patch_gradient(): lax.all_to_all(waves, ('ty', 'tx'), split_axis=0, concat_axis=0, tiled=True)]
    transpose x1, local copies, waits for them, and re-layouts: 10.5 us -> 0.15 us  [per_device(): w_unembed.reshape(D, PATCH, PATCH).transpose(0, 2, 1).reshape(D, PIXELS)]
  transfers between devices with their start and end apart: 11 -> 11, of which waited for: 10 -> 10; matrix products, arithmetic and copies ran while one was open for 12% -> 8% of each run, Pallas kernels for 0% -> 1%
where the time goes in v2:
time: 564 us; the launch traced here: 556 us
  Pallas kernels  192 us (34%)
  blocking collectives  161 us (29%)
  waiting for transfers between devices  105 us (19%)
  local copies, waits for them, and re-layouts  40.7 us (7%)
  other arithmetic  28.2 us (5%)
  starting transfers between devices  20.5 us (4%)
  between operations  8.58 us (2%)
    pallas_call x2, Pallas kernels, second_block(): pl.pallas_call(second_kernel, grid_spec=pltpu.PrefetchScalarGridSpec(num_...  56.8 us
    all_to_all x1, blocking collectives, patch_gradient(): lax.all_to_all(sent.reshape(devices, 2, slab, slab), ('ty', 'tx'), split_...  52.4 us
    all_to_all x1, blocking collectives, patch_gradient(): lax.all_to_all(waves, ('ty', 'tx'), split_axis=0, concat_axis=0, tiled=True)  52.4 us
    pallas_call x2, Pallas kernels, first_block(): pl.pallas_call(functools.partial(first_kernel, zeta), grid=(rows // WIN,)...  51.8 us
    all_to_all x1, waiting for transfers between devices, patch_gradient(): lax.all_to_all(waves, ('ty', 'tx'), split_axis=0, concat_axis=0, tiled=True)  47.6 us
    all_to_all x2, blocking collectives, patch_gradient(): lax.all_to_all(state.reshape(tx, own, cols, PIXELS), 'tx', split_axis=0,...  36.9 us
    pallas_call x2, Pallas kernels, patch_gradient(): pl.pallas_call(column_both, out_shape=jax.ShapeDtypeStruct((devices, 2, s...  33.8 us
    ppermute x8, waiting for transfers between devices, from_behind(): lax.ppermute(shard, axis, [(i, (i + by) % size) for i in range(size)])  33.3 us
  transfers between devices with their start and end apart: 11, of which 10 were waited for; matrix products, arithmetic and copies ran while one was open for 8% of the time, Pallas kernels for 1%

profile of v2, /device:TPU:0, one launch (start us, length us, event | category | flops | bytes accessed | tf_op | source)
XLA Modules:
  0.0 555.7 jit_solution(9505524765179322982)
XLA Ops:
  0.0 6.5 %shard_map.226.state_ref = f32[32,64,256]{2,1,0:T(8,128)} custom-call(f32[1,512,1024]{2,1,0:T(8,128)} %bitcast.81, bf16[1024,1024]{1,0:T(8,128)(2,1)} %constant.82.clone.order_ref), custom_call_target="tpu_custom_call" | custom-call | tf_op jit(solution)/shard_map/pallas_call | solution.py:572
  8.2 19.2 %all_to_all.40.x_ref = bf16[4,8,64,256]{3,2,1,0:T(8,128)(2,1)} all-to-all(bf16[4,8,64,256]{3,2,1,0:T(8,128)(2,1)S(1)} %bitcast.73), channel_id=1, replica_groups=mesh['ty'=8,'tx'=4] {'tx'}, dimensions={0} | all-to-all | bytes 2097152 | tf_op jit(solution)/shard_map/all_to_all | solution.py:279
  27.4 7.0 %shard_map.227 = bf16[16,2,2,128,128]{4,3,2,1,0:T(8,128)(2,1)} custom-call(bf16[4,8,64,256]{3,2,1,0:T(8,128)(2,1)} %all_to_all.40.x_ref, bf16[256,512]{1,0:T(8,128)(2,1)} %constant.83.clone.first_ref, f32[2,256,256]{2,1,0:T(8,128)} %constant.84.clone.twist_ref, bf16[512,512]{1,0:T(8,128)(2,1)} %constant.85.clone.second_ref), custom_call_target="tpu_custom_call" | custom-call | tf_op jit(solution)/shard_map/pallas_call | solution.py:282
  34.5 4.3 all-to-all-start.1
  38.8 4.7 fusion.15
  49.4 4.7 fusion.14
  62.9 5.1 fusion.1
  71.9 15.7 %all-to-all-done.1.x_ref = bf16[32,2,128,128]{3,2,1,0:T(8,128)(2,1)S(1)} async-done(((bf16[32,2,128,128]{3,2,1,0:T(8,128)(2,1)}), bf16[32,2,128,128]{3,2,1,0:T(8,128)(2,1)S(1)}, u32[]{:S(2)}, u32[]{:S(2)}) %all-to-all-start.1) | async-done | bytes 2097184 | tf_op jit(solution)/shard_map/all_to_all | solution.py:287
  88.9 16.9 %shard_map.228 = bf16[32,2,128,128]{3,2,1,0:T(8,128)(2,1)} custom-call(bf16[32,2,128,128]{3,2,1,0:T(8,128)(2,1)} %copy-done.2, bf16[32,128,128]{2,1,0:T(8,128)(2,1)} %bitcast.66, bf16[2,32,128,128]{3,2,1,0:T(8,128)(2,1)} %pad_maximum_fusion.2.data_ref, bf16[1024,1024]{1,0:T(8,128)(2,1)} %constant.87.clone.outer_ref, ...), custom_call_target="tpu_custom_call" | custom-call | tf_op jit(solution)/shard_map/pallas_call | solution.py:290
  105.8 4.4 all-to-all-start.2
  111.3 47.6 %all-to-all-done.2 = bf16[32,2,128,128]{3,2,1,0:T(8,128)(2,1)S(1)} async-done(((bf16[32,2,128,128]{3,2,1,0:T(8,128)(2,1)}), bf16[32,2,128,128]{3,2,1,0:T(8,128)(2,1)S(1)}, u32[]{:S(2)}, u32[]{:S(2)}) %all-to-all-start.2) | async-done | bytes 2097184 | tf_op jit(solution)/shard_map/all_to_all | solution.py:296
  160.2 7.9 %shard_map.229 = bf16[4,8,64,256]{3,2,1,0:T(8,128)(2,1)} custom-call(bf16[16,2,2,128,128]{4,3,2,1,0:T(8,128)(2,1)} %bitcast.69, bf16[256,512]{1,0:T(8,128)(2,1)} %constant.83.clone.first_ref, f32[2,256,256]{2,1,0:T(8,128)} %constant.84.clone.twist_ref, bf16[512,512]{1,0:T(8,128)(2,1)} %constant.86.clone.second_ref), custom_call_target="tpu_custom_call" | custom-call | tf_op jit(solution)/shard_map/pallas_call | solution.py:297
  168.1 4.0 all-to-all-start.3
  177.2 8.4 %all-to-all-done.3 = bf16[4,8,64,256]{3,2,1,0:T(8,128)(2,1)S(1)} async-done(((bf16[4,8,64,256]{3,2,1,0:T(8,128)(2,1)}), bf16[4,8,64,256]{3,2,1,0:T(8,128)(2,1)S(1)}, u32[]{:S(2)}, u32[]{:S(2)}) %all-to-all-start.3) | async-done | bytes 1048608 | tf_op jit(solution)/shard_map/all_to_all | solution.py:302
  186.6 25.9 %shard_map.230 = (f32[32,64,256]{2,1,0:T(8,128)}, bf16[32,64,512]{2,1,0:T(8,128)(2,1)}) custom-call(f32[32,64,256]{2,1,0:T(8,128)} %shard_map.226.state_ref, bf16[32,64,256]{2,1,0:T(8,128)(2,1)} %bitcast.77, f32[32,64,128]{2,1,0:T(8,128)} %pad_maximum_fusion.3.bias_ref, bf16[256,512]{1,0:T(8,128)(2,1)} %bitcast.79, bf16[2,512,1536]{2,1,0:T(8,128)(2,1)} %qkv_ref.7, ...), custom_call_target="tpu_custom_call" | custom-call | tf_op jit(solution)/shard_map/pallas_call | solution.py:444
  216.7 4.3 collective-permute-done
  223.5 5.2 collective-permute-done.1
  230.6 28.4 %shard_map.231 = bf16[32,64,256]{2,1,0:T(8,128)(2,1)} custom-call(s32[2]{0:T(128)} %get-tuple-element.23.shift_ref, bf16[40,72,512]{2,1,0:T(8,128)(2,1)} %pad_maximum_fusion.grid_ref, f32[32,64,128]{2,1,0:T(8,128)} %pad_maximum_fusion.4.bias_ref, bf16[2,512,1536]{2,1,0:T(8,128)(2,1)} %qkv_ref.7, bf16[2,512,512]{2,1,0:T(8,128)(2,1)} %proj_ref.7, ...), custom_call_target="tpu_custom_call" | custom-call | tf_op jit(solution)/shard_map/pallas_call | solution.py:460
  261.9 5.2 collective-permute-done.2
  271.8 6.6 %shard_map.232 = f32[32,64,256]{2,1,0:T(8,128)} custom-call(f32[2,512,1024]{2,1,0:T(8,128)} %noise_ref.1, bf16[1024,1024]{1,0:T(8,128)(2,1)} %constant.82.clone.order_ref), custom_call_target="tpu_custom_call" | custom-call | tf_op jit(solution)/shard_map/pallas_call | solution.py:572
  282.3 17.7 %all_to_all.41.x_ref = bf16[4,8,64,256]{3,2,1,0:T(8,128)(2,1)} all-to-all(bf16[4,8,64,256]{3,2,1,0:T(8,128)(2,1)S(1)} %bitcast.72), channel_id=1, replica_groups=mesh['ty'=8,'tx'=4] {'tx'}, dimensions={0} | all-to-all | bytes 2097152 | tf_op jit(solution)/shard_map/all_to_all | solution.py:279
  300.0 7.0 %shard_map.233 = bf16[16,2,2,128,128]{4,3,2,1,0:T(8,128)(2,1)} custom-call(bf16[4,8,64,256]{3,2,1,0:T(8,128)(2,1)} %all_to_all.41.x_ref, bf16[256,512]{1,0:T(8,128)(2,1)} %constant.83.clone.first_ref, f32[2,256,256]{2,1,0:T(8,128)} %constant.84.clone.twist_ref, bf16[512,512]{1,0:T(8,128)(2,1)} %constant.85.clone.second_ref), custom_call_target="tpu_custom_call" | custom-call | tf_op jit(solution)/shard_map/pallas_call | solution.py:282
  307.1 52.4 %all_to_all.42.x_ref = bf16[32,2,128,128]{3,2,1,0:T(8,128)(2,1)} all-to-all(bf16[32,2,128,128]{3,2,1,0:T(8,128)(2,1)} %bitcast.71), channel_id=1, replica_groups=mesh['ty'=8,'tx'=4] {'ty','tx'}, dimensions={0} | all-to-all | bytes 4194304 | tf_op jit(solution)/shard_map/all_to_all | solution.py:287
  359.5 16.9 %shard_map.234 = bf16[32,2,128,128]{3,2,1,0:T(8,128)(2,1)} custom-call(bf16[32,2,128,128]{3,2,1,0:T(8,128)(2,1)} %all_to_all.42.x_ref, bf16[32,128,128]{2,1,0:T(8,128)(2,1)} %bitcast.67, bf16[2,32,128,128]{3,2,1,0:T(8,128)(2,1)} %pad_maximum_fusion.2.data_ref, bf16[1024,1024]{1,0:T(8,128)(2,1)} %constant.87.clone.outer_ref, ...), custom_call_target="tpu_custom_call" | custom-call | tf_op jit(solution)/shard_map/pallas_call | solution.py:290
  376.4 52.4 %all_to_all.43 = bf16[32,2,128,128]{3,2,1,0:T(8,128)(2,1)} all-to-all(bf16[32,2,128,128]{3,2,1,0:T(8,128)(2,1)} %shard_map.234), channel_id=1, replica_groups=mesh['ty'=8,'tx'=4] {'ty','tx'}, dimensions={0} | all-to-all | bytes 4194304 | tf_op jit(solution)/shard_map/all_to_all | solution.py:296
  428.8 7.9 %shard_map.235 = bf16[4,8,64,256]{3,2,1,0:T(8,128)(2,1)} custom-call(bf16[16,2,2,128,128]{4,3,2,1,0:T(8,128)(2,1)} %bitcast.70, bf16[256,512]{1,0:T(8,128)(2,1)} %constant.83.clone.first_ref, f32[2,256,256]{2,1,0:T(8,128)} %constant.84.clone.twist_ref, bf16[512,512]{1,0:T(8,128)(2,1)} %constant.86.clone.second_ref), custom_call_target="tpu_custom_call" | custom-call | tf_op jit(solution)/shard_map/pallas_call | solution.py:297
  436.7 18.8 %all_to_all.44 = bf16[4,8,64,256]{3,2,1,0:T(8,128)(2,1)} all-to-all(bf16[4,8,64,256]{3,2,1,0:T(8,128)(2,1)} %shard_map.235), channel_id=1, replica_groups=mesh['ty'=8,'tx'=4] {'tx'}, dimensions={0} | all-to-all | bytes 2097152 | tf_op jit(solution)/shard_map/all_to_all | solution.py:302
  455.4 25.9 %shard_map.236 = (f32[32,64,256]{2,1,0:T(8,128)}, bf16[32,64,512]{2,1,0:T(8,128)(2,1)}) custom-call(f32[32,64,256]{2,1,0:T(8,128)} %get-tuple-element.14.state_ref, bf16[32,64,256]{2,1,0:T(8,128)(2,1)} %bitcast.78, f32[32,64,128]{2,1,0:T(8,128)} %pad_maximum_fusion.3.bias_ref, bf16[256,512]{1,0:T(8,128)(2,1)} %bitcast.80, bf16[2,512,1536]{2,1,0:T(8,128)(2,1)} %qkv_ref.7, ...), custom_call_target="tpu_custom_call" | custom-call | tf_op jit(solution)/shard_map/pallas_call | solution.py:444
  498.6 28.5 %shard_map.237 = bf16[32,64,256]{2,1,0:T(8,128)(2,1)} custom-call(s32[2]{0:T(128)} %get-tuple-element.22.shift_ref, bf16[40,72,512]{2,1,0:T(8,128)(2,1)} %pad_maximum_fusion.1.grid_ref, f32[32,64,128]{2,1,0:T(8,128)} %pad_maximum_fusion.5.bias_ref, bf16[2,512,1536]{2,1,0:T(8,128)(2,1)} %qkv_ref.7, bf16[2,512,512]{2,1,0:T(8,128)(2,1)} %proj_ref.7, ...), custom_call_target="tpu_custom_call" | custom-call | tf_op jit(solution)/shard_map/pallas_call | solution.py:460
  530.3 5.1 collective-permute-done.6
  539.8 5.6 %collective-permute-done.7 = bf16[8,72,256]{2,1,0:T(8,128)(2,1)} collective-permute-done((bf16[8,72,256]{2,1,0:T(8,128)(2,1)}, bf16[8,72,256]{2,1,0:T(8,128)(2,1)}, u32[]{:S(2)}, u32[]{:S(2)}) %collective-permute-start.7) | collective-permute-done | bytes 294944 | tf_op jit(solution)/shard_map/ppermute | solution.py:478
  548.3 6.9 %shard_map.238 = f32[512,1024]{1,0:T(8,128)} custom-call(f32[32,64,256]{2,1,0:T(8,128)} %multiply_subtract_fusion.patch_ref, f32[2,512,1024]{2,1,0:T(8,128)} %noise_ref.1, bf16[1024,1024]{1,0:T(8,128)(2,1)} %constant.91.clone.order_ref), custom_call_target="tpu_custom_call" | custom-call | tf_op jit(solution)/shard_map/pallas_call | solution.py:589
  (83 shorter events, 70.1 us)
Async XLA Ops:
  34.5 53.0 %all-to-all-start.1 = ((bf16[32,2,128,128]{3,2,1,0:T(8,128)(2,1)}), bf16[32,2,128,128]{3,2,1,0:T(8,128)(2,1)S(1)}, u32[]{:S(2)}, u32[]{:S(2)}) async-start(bf16[32,2,128,128]{3,2,1,0:T(8,128)(2,1)} %bitcast.68), calls=%async_computation.1 | async-start | bytes 4194304 | tf_op jit(solution)/shard_map/all_to_all | solution.py:287
  87.5 1.3 copy-start.2
  105.8 4.4 copy-start.10
  105.8 4.7 copy-start.8
  105.8 53.1 %all-to-all-start.2 = ((bf16[32,2,128,128]{3,2,1,0:T(8,128)(2,1)}), bf16[32,2,128,128]{3,2,1,0:T(8,128)(2,1)S(1)}, u32[]{:S(2)}, u32[]{:S(2)}) async-start(bf16[32,2,128,128]{3,2,1,0:T(8,128)(2,1)} %shard_map.228), calls=%async_computation.2 | async-start | bytes 4194304 | tf_op jit(solution)/shard_map/all_to_all | solution.py:296
  158.9 1.3 copy-start.3
  168.1 4.0 copy-start.11
  168.1 17.5 %all-to-all-start.3 = ((bf16[4,8,64,256]{3,2,1,0:T(8,128)(2,1)}), bf16[4,8,64,256]{3,2,1,0:T(8,128)(2,1)S(1)}, u32[]{:S(2)}, u32[]{:S(2)}) async-start(bf16[4,8,64,256]{3,2,1,0:T(8,128)(2,1)} %shard_map.229), calls=%async_computation.3 | async-start | bytes 2097152 | tf_op jit(solution)/shard_map/all_to_all | solution.py:302
  185.6 1.0 copy-start.4
  186.6 28.7 %copy-start.9 = (bf16[512,256]{1,0:T(8,128)(2,1)S(1)}, bf16[512,256]{1,0:T(8,128)(2,1)}, u32[]{:S(2)}) copy-start(bf16[512,256]{1,0:T(8,128)(2,1)} %param.36) | copy-start | bytes 786436
  212.5 4.0 copy-start.5
  213.6 7.3 %collective-permute-start = (bf16[32,8,512]{2,1,0:T(8,128)(2,1)S(1)}, bf16[32,8,512]{2,1,0:T(8,128)(2,1)S(1)}, u32[]{:S(2)}, u32[]{:S(2)}) collective-permute-start(bf16[32,8,512]{2,1,0:T(8,128)(2,1)S(1)} %slice.61), channel_id=1, source_target_pairs={{0,3},{1,0},{2,1},{3,2},{4,7},{5,4},{6,5},{7,6},{8,11},{9,8},{10,9... | collective-permute-start | bytes 786440 | tf_op jit(solution)/shard_map/ppermute | solution.py:478
  221.0 7.7 %collective-permute-start.1 = (bf16[8,72,512]{2,1,0:T(8,128)(2,1)S(1)}, bf16[8,72,512]{2,1,0:T(8,128)(2,1)S(1)}, u32[]{:S(2)}, u32[]{:S(2)}) collective-permute-start(bf16[8,72,512]{2,1,0:T(8,128)(2,1)S(1)} %slice.74), channel_id=1, source_target_pairs={{0,28},{4,0},{8,4},{12,8},{16,12},{20,16},{24,20},{28,24},{1,29},{... | collective-permute-start | bytes 1769480 | tf_op jit(solution)/shard_map/ppermute | solution.py:478
  259.8 7.3 %collective-permute-start.2 = (bf16[32,8,256]{2,1,0:T(8,128)(2,1)S(1)}, bf16[32,8,256]{2,1,0:T(8,128)(2,1)S(1)}, u32[]{:S(2)}, u32[]{:S(2)}) collective-permute-start(bf16[32,8,256]{2,1,0:T(8,128)(2,1)S(1)} %slice.75), channel_id=1, source_target_pairs={{0,1},{1,2},{2,3},{3,0},{4,5},{5,6},{6,7},{7,4},{8,9},{9,10},{10,1... | collective-permute-start | bytes 393224 | tf_op jit(solution)/shard_map/ppermute | solution.py:478
  268.8 9.6 %collective-permute-start.3 = (bf16[8,72,256]{2,1,0:T(8,128)(2,1)}, bf16[8,72,256]{2,1,0:T(8,128)(2,1)}, u32[]{:S(2)}, u32[]{:S(2)}) collective-permute-start(bf16[8,72,256]{2,1,0:T(8,128)(2,1)} %pad_maximum_fusion.7), channel_id=1, source_target_pairs={{0,4},{4,8},{8,12},{12,16},{16,20},{20,24},{24,28},{28,0},{1,5},{5... | collective-permute-start | bytes 884744 | tf_op jit(solution)/shard_map/ppermute | solution.py:478
  271.7 6.7 %copy-start = (bf16[32,64,256]{2,1,0:T(8,128)(2,1)S(1)}, bf16[32,64,256]{2,1,0:T(8,128)(2,1)}, u32[]{:S(2)}) copy-start(bf16[32,64,256]{2,1,0:T(8,128)(2,1)} %shard_map.231) | copy-start | bytes 3145732
  271.8 6.7 %copy-start.6 = (f32[32,64,256]{2,1,0:T(8,128)S(1)}, f32[32,64,256]{2,1,0:T(8,128)}, u32[]{:S(2)}) copy-start(f32[32,64,256]{2,1,0:T(8,128)} %get-tuple-element.9) | copy-start | bytes 6291460
  482.3 6.7 %collective-permute-start.4 = (bf16[32,8,512]{2,1,0:T(8,128)(2,1)S(1)}, bf16[32,8,512]{2,1,0:T(8,128)(2,1)S(1)}, u32[]{:S(2)}, u32[]{:S(2)}) collective-permute-start(bf16[32,8,512]{2,1,0:T(8,128)(2,1)S(1)} %slice.68), channel_id=1, source_target_pairs={{0,3},{1,0},{2,1},{3,2},{4,7},{5,4},{6,5},{7,6},{8,11},{9,8},{10,9... | collective-permute-start | bytes 786440 | tf_op jit(solution)/shard_map/ppermute | solution.py:478
  489.0 7.7 %collective-permute-start.5 = (bf16[8,72,512]{2,1,0:T(8,128)(2,1)S(1)}, bf16[8,72,512]{2,1,0:T(8,128)(2,1)S(1)}, u32[]{:S(2)}, u32[]{:S(2)}) collective-permute-start(bf16[8,72,512]{2,1,0:T(8,128)(2,1)S(1)} %slice.76), channel_id=1, source_target_pairs={{0,28},{4,0},{8,4},{12,8},{16,12},{20,16},{24,20},{28,24},{1,29},{... | collective-permute-start | bytes 1769480 | tf_op jit(solution)/shard_map/ppermute | solution.py:478
  498.6 46.7 %copy-start.7 = (f32[32,64,256]{2,1,0:T(8,128)S(1)}, f32[32,64,256]{2,1,0:T(8,128)}, u32[]{:S(2)}) copy-start(f32[32,64,256]{2,1,0:T(8,128)} %get-tuple-element.11) | copy-start | bytes 6291460
  527.1 18.3 %copy-start.1 = (bf16[32,64,256]{2,1,0:T(8,128)(2,1)S(1)}, bf16[32,64,256]{2,1,0:T(8,128)(2,1)}, u32[]{:S(2)}) copy-start(bf16[32,64,256]{2,1,0:T(8,128)(2,1)} %shard_map.237) | copy-start | bytes 3145732
  528.1 7.3 %collective-permute-start.6 = (bf16[32,8,256]{2,1,0:T(8,128)(2,1)S(1)}, bf16[32,8,256]{2,1,0:T(8,128)(2,1)S(1)}, u32[]{:S(2)}, u32[]{:S(2)}) collective-permute-start(bf16[32,8,256]{2,1,0:T(8,128)(2,1)S(1)} %slice.77), channel_id=1, source_target_pairs={{0,1},{1,2},{2,3},{3,0},{4,5},{5,6},{6,7},{7,4},{8,9},{9,10},{10,1... | collective-permute-start | bytes 393224 | tf_op jit(solution)/shard_map/ppermute | solution.py:478
  537.1 8.3 %collective-permute-start.7 = (bf16[8,72,256]{2,1,0:T(8,128)(2,1)}, bf16[8,72,256]{2,1,0:T(8,128)(2,1)}, u32[]{:S(2)}, u32[]{:S(2)}) collective-permute-start(bf16[8,72,256]{2,1,0:T(8,128)(2,1)} %pad_maximum_fusion.6), channel_id=1, source_target_pairs={{0,4},{4,8},{8,12},{12,16},{16,20},{20,24},{24,28},{28,0},{1,5},{5... | collective-permute-start | bytes 884744 | tf_op jit(solution)/shard_map/ppermute | solution.py:478

commit v3 on v2

--- a/solution.py
+++ b/solution.py
@@ -19,6 +19,7 @@
 STEPS = 2
 SPAN = WIN * WIN
 LANES = 128
+CHUNKS = 2
 TOK = N // PATCH
 
 SIGMAS = (0.8, 0.5, 0.3)
@@ -213,39 +214,105 @@
     lax.fori_loop(0, count, step, 0)
 
 
-def column_both(
-    x_ref, scale_ref, data_ref, outer_ref, outer_t_ref, inner_ref, inner_t_ref, out_ref, mid_ref
-):
-    devices, _, rows, width = x_ref.shape
-    wide = devices * 2 * PATCH
-
-    def turn(source, target, matrix):
-        for pair in range(rows // (2 * PATCH)):
-            first = slice(pair * 2 * PATCH, pair * 2 * PATCH + PATCH)
-            second = slice(pair * 2 * PATCH + PATCH, (pair + 1) * 2 * PATCH)
-            both = jnp.concatenate(
-                [
-                    source[:, :, first, :].reshape(wide, width),
-                    source[:, :, second, :].reshape(wide, width),
-                ],
-                axis=1,
+def row_places(devices, rows, lanes, chunks):
+    across = devices // lanes
+    tile = N // across
+    places = []
+    for group in range(rows // PATCH):
+        place = []
+        for high in range(devices):
+            ty, rest = divmod(high * rows + group * PATCH, tile)
+            chunk, rest = divmod(rest, tile // chunks)
+            tx, rest = divmod(rest, tile // chunks // lanes)
+            place.append((chunk, ty * lanes + tx, rest))
+        places.append(place)
+    return places
+
+
+def column_both(places, chunks, phased, *refs):
+    x_refs, refs = refs[:chunks], refs[chunks:]
+    if phased:
+        phase_ref, refs = refs[0], refs[1:]
+    outer_ref, inner_hbm, scale_hbm, data_hbm, inner_t_hbm, outer_t_hbm = refs[:6]
+    out_refs, refs = refs[6 : 6 + chunks], refs[6 + chunks :]
+    mid_ref, inner_ref, scale_ref, data_ref, inner_t_ref, outer_t_ref, sems = refs
+    devices, _, rows, width = mid_ref.shape
+    copies = [
+        pltpu.make_async_copy(source, target, sems.at[n])
+        for n, (source, target) in enumerate(
+            (
+                (inner_hbm, inner_ref),
+                (scale_hbm, scale_ref),
+                (data_hbm, data_ref),
+                (inner_t_hbm, inner_t_ref),
+                (outer_t_hbm, outer_t_ref),
             )
-            result = mm(matrix[...], both).astype(BF16)
-            target[:, :, first, :] = result[:, :width].reshape(devices, 2, PATCH, width)
-            target[:, :, second, :] = result[:, width:].reshape(devices, 2, PATCH, width)
-
-    turn(x_ref, mid_ref, outer_ref)
+        )
+    ]
+    for copy in copies:
+        copy.start()
+    span = 2 * PATCH
+
+    for pair in range(len(places) // 2):
+        groups = (2 * pair, 2 * pair + 1)
+        both = jnp.concatenate(
+            [
+                jnp.concatenate(
+                    [
+                        x_refs[m][source, :, row : row + PATCH, :].reshape(span, width)
+                        for m, source, row in places[group]
+                    ],
+                    axis=0,
+                )
+                for group in groups
+            ],
+            axis=1,
+        )
+        result = mm(outer_ref[...], both).astype(BF16)
+        for n, group in enumerate(groups):
+            mid_ref[:, :, group * PATCH : (group + 1) * PATCH, :] = result[
+                :, n * width : (n + 1) * width
+            ].reshape(devices, 2, PATCH, width)
+
+    for copy in copies[:4]:
+        copy.wait()
 
     def step(q, carry):
-        spectrum = mm(inner_ref[q], mid_ref[q].reshape(2 * rows, width)).reshape(2, rows, width)
+        spectrum = mm(inner_ref[q], mid_ref[q].reshape(2 * rows, width))
+        real, imag = spectrum[:rows], spectrum[rows:]
+        if phased:
+            pr, pi = phase_ref[q, 0], phase_ref[q, 1]
+            real = real.reshape(rows // 8, 8, width)
+            imag = imag.reshape(rows // 8, 8, width)
+            real, imag = real * pr - imag * pi, real * pi + imag * pr
+            real, imag = real.reshape(rows, width), imag.reshape(rows, width)
         scale = scale_ref[q].astype(F32)
-        back = spectrum * scale[None] - data_ref[:, q].astype(F32)
-        wave = mm(inner_t_ref[q], back.astype(BF16).reshape(2 * rows, width))
-        mid_ref[q] = wave.astype(BF16).reshape(2, rows, width)
+        real = real * scale - data_ref[0, q].astype(F32)
+        imag = imag * scale - data_ref[1, q].astype(F32)
+        back = jnp.concatenate([real.astype(BF16), imag.astype(BF16)], axis=0)
+        mid_ref[q] = mm(inner_t_ref[q], back).astype(BF16).reshape(2, rows, width)
         return carry
 
-    lax.fori_loop(0, devices, step, 0, unroll=4)
-    turn(mid_ref, out_ref, outer_t_ref)
+    lax.fori_loop(0, devices, step, 0, unroll=8)
+    copies[4].wait()
+
+    for pair in range(len(places) // 2):
+        groups = (2 * pair, 2 * pair + 1)
+        both = jnp.concatenate(
+            [
+                mid_ref[:, :, group * PATCH : (group + 1) * PATCH, :].reshape(
+                    devices * span, width
+                )
+                for group in groups
+            ],
+            axis=1,
+        )
+        result = mm(outer_t_ref[...], both).astype(BF16)
+        for n, group in enumerate(groups):
+            for high, (m, source, row) in enumerate(places[group]):
+                out_refs[m][source, :, row : row + PATCH, :] = result[
+                    high * span : (high + 1) * span, n * width : (n + 1) * width
+                ].reshape(2, PATCH, width)
 
 
 def spectrum_inputs(gains, observed, vis_weight, devices):
@@ -266,41 +333,78 @@
     return scale, data
 
 
-def patch_gradient(state, scale, data):
-    ty, tx = lax.axis_size("ty"), lax.axis_size("tx")
-    devices = ty * tx
-    rows, cols, _ = state.shape
-    own = rows // tx
+def row_matrix(shift):
+    first = row_constants()[0]
+    if shift is None:
+        return jnp.asarray(first)
+    twice = jnp.asarray(np.concatenate([first, first[: 2 * WIN]], axis=0))
+    return lax.dynamic_slice(twice, (shift, jnp.zeros((), jnp.int32)), first.shape)
+
+
+def phase_table(shift, devices, width):
+    kr = counting(devices)[:, None] + devices * counting(8)[None, :]
+    angle = 2.0 * math.pi / TOK * (kr * shift % TOK).astype(F32)
+    table = jnp.stack([jnp.cos(angle), -jnp.sin(angle)], axis=1)
+    return jnp.broadcast_to(table[..., None], (devices, 2, 8, width))
+
+
+def patch_gradient(chunks, scale, data, shift):
+    lanes = lax.axis_size("tx")
+    devices = lax.axis_size("ty") * lanes
+    rows, cols, _ = chunks[0].shape
+    count = len(chunks)
+    own = rows // lanes
     slab = N // devices
     first, twist, second, second_t = (jnp.asarray(value) for value in row_constants())
     outer, outer_t, inner, inner_t = (
         jnp.asarray(value) for value in column_constants(devices, slab)
     )
-    gathered = lax.all_to_all(
-        state.reshape(tx, own, cols, PIXELS), "tx", split_axis=0, concat_axis=0, tiled=True
-    )
-    sent = pl.pallas_call(
-        row_forward,
-        out_shape=jax.ShapeDtypeStruct((PATCH, devices // PATCH, 2, slab, slab), BF16),
+    start = row_matrix(None if shift is None else shift[1])
+    part = (devices, 2, own * PATCH, slab)
+    split = (PATCH, devices // PATCH) + part[1:]
+    moved = []
+    for chunk in chunks:
+        gathered = lax.all_to_all(
+            chunk.reshape(lanes, own, cols, PIXELS), "tx", split_axis=0, concat_axis=0, tiled=True
+        )
+        sent = pl.pallas_call(
+            row_forward,
+            out_shape=jax.ShapeDtypeStruct(split, BF16),
+            compiler_params=PARAMS,
+        )(gathered, start, twist, second)
+        moved.append(
+            lax.all_to_all(
+                sent.reshape(part), ("ty", "tx"), split_axis=0, concat_axis=0, tiled=True
+            )
+        )
+    operands = list(moved)
+    if shift is not None:
+        operands.append(phase_table(shift[0], devices, slab))
+    held = len(operands) + 1
+    away = (inner, scale, data, inner_t, outer_t)
+    waves = pl.pallas_call(
+        functools.partial(
+            column_both, row_places(devices, slab, lanes, count), count, shift is not None
+        ),
+        in_specs=[pl.BlockSpec(memory_space=pltpu.VMEM)] * held
+        + [pl.BlockSpec(memory_space=pl.ANY)] * len(away),
+        out_shape=[jax.ShapeDtypeStruct(part, BF16)] * count,
+        scratch_shapes=[pltpu.VMEM((devices, 2, slab, slab), BF16)]
+        + [pltpu.VMEM(value.shape, BF16) for value in away]
+        + [pltpu.SemaphoreType.DMA((len(away),))],
         compiler_params=PARAMS,
-    )(gathered, first, twist, second)
-    moved = lax.all_to_all(
-        sent.reshape(devices, 2, slab, slab), ("ty", "tx"), split_axis=0, concat_axis=0, tiled=True
-    )
-    waves = pl.pallas_call(
-        column_both,
-        out_shape=jax.ShapeDtypeStruct((devices, 2, slab, slab), BF16),
-        scratch_shapes=[pltpu.VMEM((devices, 2, slab, slab), BF16)],
-        compiler_params=PARAMS,
-    )(moved, scale, data, outer, outer_t, inner, inner_t)
-    returned = lax.all_to_all(waves, ("ty", "tx"), split_axis=0, concat_axis=0, tiled=True)
-    slabs = pl.pallas_call(
-        row_inverse,
-        out_shape=jax.ShapeDtypeStruct((tx, own, cols, PIXELS), BF16),
-        compiler_params=PARAMS,
-    )(returned.reshape(PATCH, devices // PATCH, 2, slab, slab), first, twist, second_t)
-    grad = lax.all_to_all(slabs, "tx", split_axis=0, concat_axis=0, tiled=True)
-    return grad.reshape(rows, cols, PIXELS)
+    )(*operands, outer, *away)
+    grads = []
+    for wave in waves:
+        returned = lax.all_to_all(wave, ("ty", "tx"), split_axis=0, concat_axis=0, tiled=True)
+        slabs = pl.pallas_call(
+            row_inverse,
+            out_shape=jax.ShapeDtypeStruct((lanes, own, cols, PIXELS), BF16),
+            compiler_params=PARAMS,
+        )(returned.reshape(split), first, twist, second_t)
+        grad = lax.all_to_all(slabs, "tx", split_axis=0, concat_axis=0, tiled=True)
+        grads.append(grad.reshape(rows, cols, PIXELS))
+    return grads
 
 
 def layer_norm(values, gain):
@@ -379,24 +483,30 @@
     return flow + 0.5 * total
 
 
-def first_kernel(
-    zeta, state_ref, grad_ref, bias_ref, embed_ref, qkv_ref, proj_ref, up_ref, down_ref, gain_ref,
-    half_ref, out_ref, mixed_ref, score_ref, prob_ref,
-):
+def first_kernel(zeta, sigma, *refs):
+    state_ref, grad_ref = refs[:2]
+    refs = refs[2:]
+    if sigma is not None:
+        noise_ref, refs = refs[0], refs[1:]
+    bias_ref, embed_ref, qkv_ref, proj_ref, up_ref, down_ref, gain_ref = refs[:7]
+    base_ref, out_ref, *scratch = refs[7:]
     half = state_ref[...] - zeta * grad_ref[...].astype(F32)
-    half_ref[...] = half
     tokens = mm(to_windows(half).astype(BF16), embed_ref[...]).astype(BF16).astype(F32)
-    flow = swin_band(
-        tokens, bias_ref, qkv_ref, proj_ref, up_ref, down_ref, gain_ref, mixed_ref, score_ref,
-        prob_ref,
-    )
-    out_ref[...] = from_windows(flow, half.shape[1]).astype(BF16)
-
-
-def second_kernel(
-    shift_ref, grid_ref, bias_ref, qkv_ref, proj_ref, up_ref, down_ref, gain_ref, unembed_ref,
-    out_ref, mixed_ref, score_ref, prob_ref,
-):
+    if sigma is None:
+        base_ref[...] = half
+    else:
+        base = half + sigma * noise_ref[...]
+        base_ref[...] = base
+        out_ref[:, :, D:] = base.astype(BF16)
+    flow = swin_band(tokens, bias_ref, qkv_ref, proj_ref, up_ref, down_ref, gain_ref, *scratch)
+    out_ref[:, :, :D] = from_windows(flow, half.shape[1]).astype(BF16)
+
+
+def second_kernel(sigma, *refs):
+    shift_ref, grid_ref, bias_ref, qkv_ref, proj_ref, up_ref, down_ref, gain_ref = refs[:8]
+    unembed_ref, out_ref, *scratch = refs[8:]
+    if sigma is not None:
+        state_ref, scratch = scratch[0], scratch[1:]
     cols = out_ref.shape[1]
     top = pl.program_id(0) * WIN + shift_ref[0]
     wide = grid_ref[pl.ds(top, WIN)]
@@ -404,12 +514,12 @@
     target = lax.broadcasted_iota(jnp.int32, (cols, wide.shape[1]), 0) + shift_ref[1]
     pick = jnp.where(place == target, 1.0, 0.0).astype(BF16)
     band = jnp.stack([mm(pick, wide[n]) for n in range(WIN)])
-    flow = swin_band(
-        to_windows(band), bias_ref, qkv_ref, proj_ref, up_ref, down_ref, gain_ref, mixed_ref,
-        score_ref, prob_ref,
-    )
-    estimate = mm(flow.astype(BF16), unembed_ref[...])
-    out_ref[...] = from_windows(estimate, cols).astype(BF16)
+    tokens = to_windows(band[:, :, :D])
+    flow = swin_band(tokens, bias_ref, qkv_ref, proj_ref, up_ref, down_ref, gain_ref, *scratch)
+    estimate = from_windows(mm(flow.astype(BF16), unembed_ref[...]), cols)
+    out_ref[...] = estimate.astype(BF16)
+    if sigma is not None:
+        state_ref[...] = (band[:, :, D:] - sigma * estimate).astype(BF16)
 
 
 def whole(array):
@@ -417,6 +527,10 @@
     return pl.BlockSpec(array.shape, lambda *_: zeros)
 
 
+def band_of(step, cols):
+    return pl.BlockSpec((step, cols, PIXELS), lambda n: (n, 0, 0))
+
+
 def member(array, j):
     place = (j,) + (0,) * (array.ndim - 1)
     return pl.BlockSpec((None,) + array.shape[1:], lambda *_: place)
@@ -426,8 +540,8 @@
     return pl.BlockSpec((WIN, cols, feats), lambda n, *_: (n, 0, 0))
 
 
-def bias_spec(cols):
-    return pl.BlockSpec((cols // WIN, SPAN, 2 * SPAN), lambda n, *_: (n, 0, 0))
+def bias_spec(cols, skip):
+    return pl.BlockSpec((cols // WIN, SPAN, 2 * SPAN), lambda n, *_: (n + skip, 0, 0))
 
 
 def band_scratch(cols):
@@ -439,36 +553,41 @@
     ]
 
 
-def first_block(zeta, state, grad, bias, w_embed, weights):
+def first_block(m, zeta, sigma, state, grad, noise, bias, w_embed, weights):
     rows, cols, _ = state.shape
+    fields = [state, grad] + ([] if sigma is None else [noise])
+    feats = D if sigma is None else D + PIXELS
     return pl.pallas_call(
-        functools.partial(first_kernel, zeta),
+        functools.partial(first_kernel, zeta, sigma),
         grid=(rows // WIN,),
-        in_specs=[band_spec(cols, PIXELS), band_spec(cols, PIXELS), bias_spec(cols), whole(w_embed)]
+        in_specs=[band_spec(cols, PIXELS)] * len(fields)
+        + [bias_spec(cols, m * rows // WIN), whole(w_embed)]
         + [member(value, 0) for value in weights],
-        out_specs=[band_spec(cols, PIXELS), band_spec(cols, D)],
+        out_specs=[band_spec(cols, PIXELS), band_spec(cols, feats)],
         out_shape=[
             jax.ShapeDtypeStruct((rows, cols, PIXELS), F32),
-            jax.ShapeDtypeStruct((rows, cols, D), BF16),
+            jax.ShapeDtypeStruct((rows, cols, feats), BF16),
         ],
         scratch_shapes=band_scratch(cols),
         compiler_params=PARAMS,
-    )(state, grad, bias, w_embed, *weights)
-
-
-def second_block(shift, grid, bias, w_unembed, weights, rows, cols):
+    )(*fields, bias, w_embed, *weights)
+
+
+def second_block(m, sigma, shift, grid, bias, w_unembed, weights):
+    rows, cols = grid.shape[0] - WIN, grid.shape[1] - WIN
+    outs = 1 if sigma is None else 2
     return pl.pallas_call(
-        second_kernel,
+        functools.partial(second_kernel, sigma),
         grid_spec=pltpu.PrefetchScalarGridSpec(
             num_scalar_prefetch=1,
             grid=(rows // WIN,),
-            in_specs=[whole(grid), bias_spec(cols)]
+            in_specs=[whole(grid), bias_spec(cols, m * rows // WIN)]
             + [member(value, 1) for value in weights]
             + [whole(w_unembed)],
-            out_specs=band_spec(cols, PIXELS),
+            out_specs=[band_spec(cols, PIXELS)] * outs,
             scratch_shapes=band_scratch(cols),
         ),
-        out_shape=jax.ShapeDtypeStruct((rows, cols, PIXELS), BF16),
+        out_shape=[jax.ShapeDtypeStruct((rows, cols, PIXELS), BF16)] * outs,
         compiler_params=PARAMS,
     )(shift, grid, bias, *weights, w_unembed)
 
@@ -478,14 +597,20 @@
     return lax.ppermute(shard, axis, [(i, (i + by) % size) for i in range(size)])
 
 
-def with_next(grid):
-    wide = jnp.concatenate([grid, from_behind(grid[:, :WIN], "tx", -1)], axis=1)
-    return jnp.concatenate([wide, from_behind(wide[:WIN], "ty", -1)], axis=0)
-
-
-def with_previous(grid):
-    wide = jnp.concatenate([from_behind(grid[:, -WIN:], "tx", 1), grid], axis=1)
-    return jnp.concatenate([from_behind(wide[-WIN:], "ty", 1), wide], axis=0)
+def with_next(chunks):
+    wide = [
+        jnp.concatenate([chunk, from_behind(chunk[:, :WIN], "tx", -1)], axis=1) for chunk in chunks
+    ]
+    heads = [chunk[:WIN] for chunk in wide[1:]] + [from_behind(wide[0][:WIN], "ty", -1)]
+    return [jnp.concatenate(pair, axis=0) for pair in zip(wide, heads)]
+
+
+def with_previous(chunks):
+    wide = [
+        jnp.concatenate([from_behind(chunk[:, -WIN:], "tx", 1), chunk], axis=1) for chunk in chunks
+    ]
+    tails = [from_behind(wide[-1][-WIN:], "ty", 1)] + [chunk[-WIN:] for chunk in wide[:-1]]
+    return [jnp.concatenate(pair, axis=0) for pair in zip(tails, wide)]
 
 
 def windows_of(grid):
@@ -530,8 +655,8 @@
     return mm(high, matrix) + mm(low, matrix)
 
 
-def to_patches_kernel(tile_ref, order_ref, out_ref):
-    count, cols, _ = out_ref.shape
+def to_patches_kernel(tile_ref, order_ref, *out_refs):
+    count, cols, _ = out_refs[0].shape
     parts = LANES // cols
     groups = PATCH // parts
     ordered = move_lanes(tile_ref[...], order_ref[...])
@@ -541,9 +666,9 @@
             [band[:, g * LANES : (g + 1) * LANES] for g in range(groups)], axis=0
         )
         turned = stacked.T
-        out_ref[i] = jnp.concatenate(
-            [turned[h * cols : (h + 1) * cols] for h in range(parts)], axis=1
-        )
+        patch = jnp.concatenate([turned[h * cols : (h + 1) * cols] for h in range(parts)], axis=1)
+        for out_ref in out_refs:
+            out_ref[i] = patch.astype(out_ref.dtype)
 
 
 def to_tile_kernel(scale, patch_ref, noise_ref, order_ref, out_ref):
@@ -565,21 +690,28 @@
     out_ref[...] = moved + scale * noise_ref[...]
 
 
-def patches_of(tiles, j):
-    rows, cols = tiles.shape[1] // PATCH, tiles.shape[2] // PATCH
+def patches_of(tiles, j, chunks, narrow=False):
+    rows, cols = tiles.shape[1] // PATCH // chunks, tiles.shape[2] // PATCH
     order = jnp.asarray(lane_order(cols)[0])
-    step = rows // 4
-    return pl.pallas_call(
-        to_patches_kernel,
-        grid=(rows // step,),
-        in_specs=[
-            pl.BlockSpec((None, step * PATCH, cols * PATCH), lambda n: (j, n, 0)),
-            whole(order),
-        ],
-        out_specs=pl.BlockSpec((step, cols, PIXELS), lambda n: (n, 0, 0)),
-        out_shape=jax.ShapeDtypeStruct((rows, cols, PIXELS), F32),
-        compiler_params=PARAMS,
-    )(tiles, order)
+    step = rows // 2
+    kinds = [F32, BF16] if narrow else [F32]
+    return [
+        pl.pallas_call(
+            to_patches_kernel,
+            grid=(rows // step,),
+            in_specs=[
+                pl.BlockSpec(
+                    (None, step * PATCH, cols * PATCH),
+                    functools.partial(lambda skip, n: (j, skip + n, 0), m * (rows // step)),
+                ),
+                whole(order),
+            ],
+            out_specs=[band_of(step, cols)] * len(kinds),
+            out_shape=[jax.ShapeDtypeStruct((rows, cols, PIXELS), kind) for kind in kinds],
+            compiler_params=PARAMS,
+        )(tiles, order)
+        for m in range(chunks)
+    ]
 
 
 def tile_of(patches, scale, noise, j):
@@ -590,7 +722,7 @@
         functools.partial(to_tile_kernel, scale),
         grid=(rows // step,),
         in_specs=[
-            pl.BlockSpec((step, cols, PIXELS), lambda n: (n, 0, 0)),
+            band_of(step, cols),
             pl.BlockSpec((None, step * PATCH, cols * PATCH), lambda n: (j, n, 0)),
             whole(order),
         ],
@@ -613,33 +745,48 @@
     weights = (w_qkv, w_proj, w_up, w_down, norm_gains)
     w_embed = w_embed.reshape(PATCH, PATCH, D).transpose(1, 0, 2).reshape(PIXELS, D)
     w_unembed = w_unembed.reshape(D, PATCH, PATCH).transpose(0, 2, 1).reshape(D, PIXELS)
-    state = patches_of(image[None], 0)
+    chunks = CHUNKS
+    begin = patches_of(image[None], 0, chunks, narrow=True)
+    state = [pair[0] for pair in begin]
+    moving = [pair[1] for pair in begin]
+    shift = None
     if fast:
         scale, data = spectrum_inputs(gains, observed, vis_weight, devices)
     first_bias = bias_of(None, key_mask)
     for step in range(STEPS):
         if fast:
-            grad = patch_gradient(state.astype(BF16), scale, data)
+            grad = patch_gradient(moving, scale, data, shift)
         else:
-            grad = plain_gradient(tile_of(state, 0.0, noise, 0), gains, observed, vis_weight)
-            grad = patches_of(grad.astype(F32)[None], 0).astype(BF16)
-        half, first = first_block(STEP_SIZES[step], state, grad, first_bias, w_embed, weights)
-        shift_rows = offsets[step, 0]
-        shift_cols = offsets[step, 1]
-        labels = 3 * region(row_index, shift_rows)[:, None] + region(col_index, shift_cols)[None, :]
+            tile = tile_of(jnp.concatenate(state), 0.0, noise, 0)
+            grad = plain_gradient(tile, gains, observed, vis_weight).astype(F32)
+            grad = [part[0].astype(BF16) for part in patches_of(grad[None], 0, chunks)]
+        last = step + 1 == STEPS
+        extra = [[None]] * chunks if last else patches_of(noise, step, chunks)
+        sigma = None if last else SIGMAS[step + 1]
+        blocks = [
+            first_block(
+                m, STEP_SIZES[step], sigma, state[m], grad[m], extra[m][0], first_bias, w_embed,
+                weights,
+            )
+            for m in range(chunks)
+        ]
+        shift = offsets[step]
+        labels = 3 * region(row_index, shift[0])[:, None] + region(col_index, shift[1])[None, :]
         second_bias = bias_of(labels, None)
-        rolled = second_block(
-            offsets[step], with_next(first), second_bias, w_unembed, weights, rows, cols
-        )
-        estimate = lax.dynamic_slice(
-            with_previous(rolled),
-            (WIN - shift_rows, WIN - shift_cols, jnp.zeros((), jnp.int32)),
-            (rows, cols, PIXELS),
-        )
-        state = half - SIGMAS[step] * estimate.astype(F32)
-        if step + 1 < STEPS:
-            state = state + SIGMAS[step + 1] * patches_of(noise, step)
-    return tile_of(state, SIGMAS[STEPS], noise, STEPS - 1)
+        grids = with_next([block[1] for block in blocks])
+        rolled = [
+            second_block(
+                m, None if last else SIGMAS[step], shift, grids[m], second_bias, w_unembed, weights
+            )
+            for m in range(chunks)
+        ]
+        moving = [part[-1] for part in rolled]
+        corner = (WIN - shift[0], WIN - shift[1], jnp.zeros((), jnp.int32))
+        state = [
+            block[0] - SIGMAS[step] * lax.dynamic_slice(part, corner, block[0].shape).astype(F32)
+            for block, part in zip(blocks, with_previous([part[0] for part in rolled]))
+        ]
+    return tile_of(jnp.concatenate(state), SIGMAS[STEPS], noise, STEPS - 1)
 
 
 def solution(mesh):

time: 564 us -> 562 us (level)
  blocking collectives: 161 us -> 74.7 us
  starting transfers between devices: 20.5 us -> 74 us
  Pallas kernels: 192 us -> 217 us
  local copies, waits for them, and re-layouts: 40.7 us -> 50.4 us
  waiting for transfers between devices: 105 us -> 96.8 us
    all_to_all x4 -> x2, blocking collectives: 142 us -> 61.5 us  [patch_gradient(): lax.all_to_all(wave, ('ty', 'tx'), split_axis=0, concat_axis=0, tiled=True)]
    all_to_all x2 -> x10, starting transfers between devices: 8.71 us -> 40.4 us  [the longest x4 17.1 us: patch_gradient(): lax.all_to_all(chunk.reshape(lanes, own, cols, PIXELS), 'tx', split_axis=...]
    pallas_call x10 -> x18, Pallas kernels: 172 us -> 193 us  [the longest x4 67 us: second_block(): pl.pallas_call(functools.partial(second_kernel, sigma), grid_spec=pltpu.P...]
    all_to_all x2 -> x10, waiting for transfers between devices: 63.2 us -> 79.7 us  [the longest x4 66.2 us: patch_gradient(): lax.all_to_all(sent.reshape(part), ('ty', 'tx'), split_axis=0, concat_axi...]
    ppermute x8 -> x12, waiting for transfers between devices: 33.3 us -> 17.1 us  [from_behind(): lax.ppermute(shard, axis, [(i, (i + by) % size) for i in range(size)])]
    ppermute x8 -> x12, starting transfers between devices: 7.78 us -> 22.2 us  [from_behind(): lax.ppermute(shard, axis, [(i, (i + by) % size) for i in range(size)])]
    all_to_all x1 -> x3, waiting for transfers between devices: 8.4 us -> 0.01 us  [patch_gradient(): grad = lax.all_to_all(slabs, 'tx', split_axis=0, concat_axis=0, tiled=True)]
    all_to_all x1 -> x3, starting transfers between devices: 4.01 us -> 11.3 us  [patch_gradient(): grad = lax.all_to_all(slabs, 'tx', split_axis=0, concat_axis=0, tiled=True)]
  transfers between devices with their start and end apart: 11 -> 25, of which waited for: 10 -> 12; matrix products, arithmetic and copies ran while one was open for 8% -> 12% of each run, Pallas kernels for 1% -> 28%
where the time goes in v3:
time: 562 us; the launch traced here: 552 us
  Pallas kernels  217 us (39%)
  waiting for transfers between devices  96.8 us (17%)
  blocking collectives  74.7 us (13%)
  starting transfers between devices  74 us (13%)
  local copies, waits for them, and re-layouts  50.4 us (9%)
  other arithmetic  27.7 us (5%)
  between operations  10.7 us (2%)
    pallas_call x4, Pallas kernels, second_block(): pl.pallas_call(functools.partial(second_kernel, sigma), grid_spec=pltpu.P...  67 us
    all_to_all x4, waiting for transfers between devices, patch_gradient(): lax.all_to_all(sent.reshape(part), ('ty', 'tx'), split_axis=0, concat_axi...  66.2 us
    all_to_all x2, blocking collectives, patch_gradient(): lax.all_to_all(wave, ('ty', 'tx'), split_axis=0, concat_axis=0, tiled=True)  61.5 us
    pallas_call x4, Pallas kernels, first_block(): pl.pallas_call(functools.partial(first_kernel, zeta, sigma), grid=(rows /...  60.7 us
    pallas_call x2, Pallas kernels, patch_gradient(): pl.pallas_call(functools.partial(column_both, row_places(devices, slab, l...  27.7 us
    unnamed x68, local copies, waits for them, and re-layouts  22.8 us
    ppermute x12, starting transfers between devices, from_behind(): lax.ppermute(shard, axis, [(i, (i + by) % size) for i in range(size)])  22.2 us
    pallas_call x4, Pallas kernels, patch_gradient(): pl.pallas_call(row_inverse, out_shape=jax.ShapeDtypeStruct((lanes, own, c...  19.6 us
  transfers between devices with their start and end apart: 25, of which 12 were waited for; matrix products, arithmetic and copies ran while one was open for 12% of the time, Pallas kernels for 28%

profile of v3, /device:TPU:0, one launch (start us, length us, event | category | flops | bytes accessed | tf_op | source)
XLA Modules:
  0.0 551.7 jit_solution(8793009089907004063)
XLA Ops:
  4.4 5.2 all-to-all-start
  9.6 4.5 shard_map.237
  21.1 4.5 shard_map.236
  29.0 4.9 all-to-all-start.1
  37.8 4.5 shard_map.238
  42.3 18.0 %all-to-all-done.1.refs_0_ = bf16[32,2,64,128]{3,2,1,0:T(8,128)(2,1)S(1)} async-done(((bf16[32,2,64,128]{3,2,1,0:T(8,128)(2,1)}), bf16[32,2,64,128]{3,2,1,0:T(8,128)(2,1)S(1)}, u32[]{:S(2)}, u32[]{:S(2)}) %all-to-all-start.1) | async-done | bytes 1048608 | tf_op jit(solution)/shard_map/all_to_all | solution.py:376
  63.9 4.7 fusion.20
  81.3 4.5 fusion.1
  90.3 13.8 %shard_map.239 = (bf16[32,2,64,128]{3,2,1,0:T(8,128)(2,1)}, bf16[32,2,64,128]{3,2,1,0:T(8,128)(2,1)}) custom-call(bf16[32,2,64,128]{3,2,1,0:T(8,128)(2,1)} %copy-done.3, bf16[32,2,64,128]{3,2,1,0:T(8,128)(2,1)} %all-to-all-done.3.refs_1_, bf16[1024,1024]{1,0:T(8,128)(2,1)} %constant.102.clone.refs_2_.refs_3_, ...), custom_call_target="tpu_custom_call" | custom-call | tf_op jit(solution)/shard_map/pallas_call | solution.py:385
  104.1 31.6 %all_to_all.80 = bf16[32,2,64,128]{3,2,1,0:T(8,128)(2,1)} all-to-all(bf16[32,2,64,128]{3,2,1,0:T(8,128)(2,1)} %get-tuple-element.28), channel_id=1, replica_groups=mesh['ty'=8,'tx'=4] {'ty','tx'}, dimensions={0} | all-to-all | bytes 2097152 | tf_op jit(solution)/shard_map/all_to_all | solution.py:399
  135.6 4.9 shard_map.240
  140.5 13.2 %all_to_all.81 = bf16[4,4,64,256]{3,2,1,0:T(8,128)(2,1)} all-to-all(bf16[4,4,64,256]{3,2,1,0:T(8,128)(2,1)} %shard_map.240), channel_id=1, replica_groups=mesh['ty'=8,'tx'=4] {'tx'}, dimensions={0} | all-to-all | bytes 1048576 | tf_op jit(solution)/shard_map/all_to_all | solution.py:405
  167.2 15.3 %shard_map.242 = (f32[16,64,256]{2,1,0:T(8,128)}, bf16[16,64,768]{2,1,0:T(8,128)(2,1)}) custom-call(f32[16,64,256]{2,1,0:T(8,128)} %get-tuple-element.25.refs_0_, bf16[16,64,256]{2,1,0:T(8,128)(2,1)} %bitcast.89, f32[16,64,256]{2,1,0:T(8,128)} %shard_map.241.refs_2_, f32[32,64,128]{2,1,0:T(8,128)} %pad_maximum_fusion.6.refs_3_.refs_2_, ...), custom_call_target="tpu_custom_call" | custom-call | tf_op jit(solution)/shard_map/pallas_call | solution.py:560
  188.1 4.9 shard_map.243
  208.1 15.3 %shard_map.245 = (f32[16,64,256]{2,1,0:T(8,128)}, bf16[16,64,768]{2,1,0:T(8,128)(2,1)}) custom-call(f32[16,64,256]{2,1,0:T(8,128)} %get-tuple-element.30.refs_0_, bf16[16,64,256]{2,1,0:T(8,128)(2,1)} %bitcast.91, f32[16,64,256]{2,1,0:T(8,128)} %shard_map.244.refs_2_, f32[32,64,128]{2,1,0:T(8,128)} %pad_maximum_fusion.6.refs_3_.refs_2_, ...), custom_call_target="tpu_custom_call" | custom-call | tf_op jit(solution)/shard_map/pallas_call | solution.py:560
  234.4 16.9 %shard_map.247 = (bf16[16,64,256]{2,1,0:T(8,128)(2,1)}, bf16[16,64,256]{2,1,0:T(8,128)(2,1)}) custom-call(s32[2]{0:T(128)} %get-tuple-element.55.refs_0_, bf16[24,72,768]{2,1,0:T(8,128)(2,1)} %pad_maximum_fusion.1.refs_1_, f32[32,64,128]{2,1,0:T(8,128)} %pad_maximum_fusion.7.refs_2_, bf16[2,512,1536]{2,1,0:T(8,128)(2,1)} %refs_3_.9, ...), custom_call_target="tpu_custom_call" | custom-call | tf_op jit(solution)/shard_map/pallas_call | solution.py:579
  258.5 17.1 %shard_map.246 = (bf16[16,64,256]{2,1,0:T(8,128)(2,1)}, bf16[16,64,256]{2,1,0:T(8,128)(2,1)}) custom-call(s32[2]{0:T(128)} %get-tuple-element.55.refs_0_, bf16[24,72,768]{2,1,0:T(8,128)(2,1)} %pad_maximum_fusion.refs_1_, f32[32,64,128]{2,1,0:T(8,128)} %pad_maximum_fusion.7.refs_2_, bf16[2,512,1536]{2,1,0:T(8,128)(2,1)} %refs_3_.9, ...), custom_call_target="tpu_custom_call" | custom-call | tf_op jit(solution)/shard_map/pallas_call | solution.py:579
  286.9 5.2 all-to-all-start.9
  292.1 4.5 shard_map.249
  296.7 21.9 %all-to-all-done.9.refs_0_ = bf16[32,2,64,128]{3,2,1,0:T(8,128)(2,1)S(1)} async-done(((bf16[32,2,64,128]{3,2,1,0:T(8,128)(2,1)}), bf16[32,2,64,128]{3,2,1,0:T(8,128)(2,1)S(1)}, u32[]{:S(2)}, u32[]{:S(2)}) %all-to-all-start.9) | async-done | bytes 1048608 | tf_op jit(solution)/shard_map/all_to_all | solution.py:376
  322.8 25.6 %all-to-all-done.11.refs_1_ = bf16[32,2,64,128]{3,2,1,0:T(8,128)(2,1)S(1)} async-done(((bf16[32,2,64,128]{3,2,1,0:T(8,128)(2,1)}), bf16[32,2,64,128]{3,2,1,0:T(8,128)(2,1)S(1)}, u32[]{:S(2)}, u32[]{:S(2)}) %all-to-all-start.11) | async-done | bytes 1048608 | tf_op jit(solution)/shard_map/all_to_all | solution.py:376
  349.5 13.9 %shard_map.250 = (bf16[32,2,64,128]{3,2,1,0:T(8,128)(2,1)}, bf16[32,2,64,128]{3,2,1,0:T(8,128)(2,1)}) custom-call(bf16[32,2,64,128]{3,2,1,0:T(8,128)(2,1)} %copy-done.4, bf16[32,2,64,128]{3,2,1,0:T(8,128)(2,1)} %copy-done.5, f32[32,2,8,128]{3,2,1,0:T(8,128)} %broadcast_in_dim.67.refs_2_, bf16[1024,1024]{1,0:T(8,128)(2,1)} %constant.102.clone.refs_2_.refs_3_, ...), custom_call_target="tpu_custom_call" | custom-call | tf_op jit(solution)/shard_map/pallas_call | solution.py:385
  363.4 30.0 %all_to_all.82 = bf16[32,2,64,128]{3,2,1,0:T(8,128)(2,1)} all-to-all(bf16[32,2,64,128]{3,2,1,0:T(8,128)(2,1)} %get-tuple-element.38), channel_id=1, replica_groups=mesh['ty'=8,'tx'=4] {'ty','tx'}, dimensions={0} | all-to-all | bytes 2097152 | tf_op jit(solution)/shard_map/all_to_all | solution.py:399
  400.4 9.2 %collective-permute-done.3 = bf16[16,8,256]{2,1,0:T(8,128)(2,1)S(1)} collective-permute-done((bf16[16,8,256]{2,1,0:T(8,128)(2,1)S(1)}, bf16[16,8,256]{2,1,0:T(8,128)(2,1)S(1)}, u32[]{:S(2)}, u32[]{:S(2)}) %collective-permute-start.3) | collective-permute-done | bytes 65568 | tf_op jit(solution)/shard_map/ppermute | solution.py:597
  414.1 4.9 shard_map.251
  419.1 7.3 %all-to-all-done.14 = bf16[32,2,64,128]{3,2,1,0:T(8,128)(2,1)S(1)} async-done(((bf16[32,2,64,128]{3,2,1,0:T(8,128)(2,1)}), bf16[32,2,64,128]{3,2,1,0:T(8,128)(2,1)S(1)}, u32[]{:S(2)}, u32[]{:S(2)}) %all-to-all-start.14) | async-done | bytes 1048608 | tf_op jit(solution)/shard_map/all_to_all | solution.py:399
  433.6 4.9 shard_map.253
  442.7 15.0 %shard_map.252 = (f32[16,64,256]{2,1,0:T(8,128)}, bf16[16,64,512]{2,1,0:T(8,128)(2,1)}) custom-call(f32[16,64,256]{2,1,0:T(8,128)} %multiply_subtract_fusion.3.refs_0_, bf16[16,64,256]{2,1,0:T(8,128)(2,1)} %bitcast.92, f32[32,64,128]{2,1,0:T(8,128)} %pad_maximum_fusion.6.refs_3_.refs_2_, bf16[256,512]{1,0:T(8,128)(2,1)} %bitcast.76, ...), custom_call_target="tpu_custom_call" | custom-call | tf_op jit(solution)/shard_map/pallas_call | solution.py:560
  468.5 15.1 %shard_map.254 = (f32[16,64,256]{2,1,0:T(8,128)}, bf16[16,64,512]{2,1,0:T(8,128)(2,1)}) custom-call(f32[16,64,256]{2,1,0:T(8,128)} %multiply_subtract_fusion.2.refs_0_, bf16[16,64,256]{2,1,0:T(8,128)(2,1)} %bitcast.90, f32[32,64,128]{2,1,0:T(8,128)} %pad_maximum_fusion.6.refs_3_.refs_2_, bf16[256,512]{1,0:T(8,128)(2,1)} %bitcast.77, ...), custom_call_target="tpu_custom_call" | custom-call | tf_op jit(solution)/shard_map/pallas_call | solution.py:560
  492.9 16.4 %shard_map.255 = bf16[16,64,256]{2,1,0:T(8,128)(2,1)} custom-call(s32[2]{0:T(128)} %get-tuple-element.54.refs_0_, bf16[24,72,512]{2,1,0:T(8,128)(2,1)} %pad_maximum_fusion.4.refs_1_, f32[32,64,128]{2,1,0:T(8,128)} %pad_maximum_fusion.8.refs_2_, bf16[2,512,1536]{2,1,0:T(8,128)(2,1)} %refs_3_.9, bf16[2,512,512]{2,1,0:T(8,128)(2,1)} %refs_4_.12, ...), custom_call_target="tpu_custom_call" | custom-call | tf_op jit(solution)/shard_map/pallas_call | solution.py:579
  518.3 16.6 %shard_map.256 = bf16[16,64,256]{2,1,0:T(8,128)(2,1)} custom-call(s32[2]{0:T(128)} %get-tuple-element.54.refs_0_, bf16[24,72,512]{2,1,0:T(8,128)(2,1)} %pad_maximum_fusion.5.refs_1_, f32[32,64,128]{2,1,0:T(8,128)} %pad_maximum_fusion.8.refs_2_, bf16[2,512,1536]{2,1,0:T(8,128)(2,1)} %refs_3_.9, bf16[2,512,512]{2,1,0:T(8,128)(2,1)} %refs_4_.12, ...), custom_call_target="tpu_custom_call" | custom-call | tf_op jit(solution)/shard_map/pallas_call | solution.py:579
  544.4 6.9 %shard_map.257 = f32[512,1024]{1,0:T(8,128)} custom-call(f32[32,64,256]{2,1,0:T(8,128)} %pad_maximum_fusion.3.patch_ref, f32[2,512,1024]{2,1,0:T(8,128)} %noise_ref.1, bf16[1024,1024]{1,0:T(8,128)(2,1)} %constant.107.clone.order_ref), custom_call_target="tpu_custom_call" | custom-call | tf_op jit(solution)/shard_map/pallas_call | solution.py:721
  (175 shorter events, 160.0 us)
Async XLA Ops:
  4.4 13.2 %all-to-all-start = ((bf16[4,4,64,256]{3,2,1,0:T(8,128)(2,1)}), bf16[4,4,64,256]{3,2,1,0:T(8,128)(2,1)S(1)}, u32[]{:S(2)}, u32[]{:S(2)}) async-start(bf16[4,4,64,256]{3,2,1,0:T(8,128)(2,1)} %bitcast.98), calls=%async_computation | async-start | bytes 1048576 | tf_op jit(solution)/shard_map/all_to_all | solution.py:367
  17.6 10.6 %all-to-all-start.2 = ((bf16[4,4,64,256]{3,2,1,0:T(8,128)(2,1)}), bf16[4,4,64,256]{3,2,1,0:T(8,128)(2,1)S(1)}, u32[]{:S(2)}, u32[]{:S(2)}) async-start(bf16[4,4,64,256]{3,2,1,0:T(8,128)(2,1)} %bitcast.97), calls=%async_computation.2 | async-start | bytes 1048576 | tf_op jit(solution)/shard_map/all_to_all | solution.py:367
  29.0 31.3 %all-to-all-start.1 = ((bf16[32,2,64,128]{3,2,1,0:T(8,128)(2,1)}), bf16[32,2,64,128]{3,2,1,0:T(8,128)(2,1)S(1)}, u32[]{:S(2)}, u32[]{:S(2)}) async-start(bf16[32,2,64,128]{3,2,1,0:T(8,128)(2,1)} %bitcast.83), calls=%async_computation.1 | async-start | bytes 2097152 | tf_op jit(solution)/shard_map/all_to_all | solution.py:376
  60.3 30.0 %all-to-all-start.3 = ((bf16[32,2,64,128]{3,2,1,0:T(8,128)(2,1)}), bf16[32,2,64,128]{3,2,1,0:T(8,128)(2,1)}, u32[]{:S(2)}, u32[]{:S(2)}) async-start(bf16[32,2,64,128]{3,2,1,0:T(8,128)(2,1)} %bitcast.81), calls=%async_computation.3 | async-start | bytes 2097152 | tf_op jit(solution)/shard_map/all_to_all | solution.py:376
  153.7 33.4 %all-to-all-start.6 = ((bf16[32,2,64,128]{3,2,1,0:T(8,128)(2,1)}), bf16[32,2,64,128]{3,2,1,0:T(8,128)(2,1)S(1)}, u32[]{:S(2)}, u32[]{:S(2)}) async-start(bf16[32,2,64,128]{3,2,1,0:T(8,128)(2,1)} %get-tuple-element.31), calls=%async_computation.6 | async-start | bytes 2097152 | tf_op jit(solution)/shard_map/all_to_all | solution.py:399
  184.1 13.9 %collective-permute-start.1 = (bf16[16,8,768]{2,1,0:T(8,128)(2,1)}, bf16[16,8,768]{2,1,0:T(8,128)(2,1)S(1)}, u32[]{:S(2)}, u32[]{:S(2)}) collective-permute-start(bf16[16,8,768]{2,1,0:T(8,128)(2,1)} %slice.100), channel_id=1, source_target_pairs={{0,3},{1,0},{2,1},{3,2},{4,7},{5,4},{6,5},{7,6},{8,11},{9,8},{10,9... | collective-permute-start | bytes 589832 | tf_op jit(solution)/shard_map/ppermute | solution.py:597
  193.0 14.2 %all-to-all-start.7 = ((bf16[4,4,64,256]{3,2,1,0:T(8,128)(2,1)}), bf16[4,4,64,256]{3,2,1,0:T(8,128)(2,1)S(1)}, u32[]{:S(2)}, u32[]{:S(2)}) async-start(bf16[4,4,64,256]{3,2,1,0:T(8,128)(2,1)} %shard_map.243), calls=%async_computation.7 | async-start | bytes 1048576 | tf_op jit(solution)/shard_map/all_to_all | solution.py:405
  199.1 56.5 %collective-permute-start.2 = (bf16[8,72,768]{2,1,0:T(8,128)(2,1)}, bf16[8,72,768]{2,1,0:T(8,128)(2,1)}, u32[]{:S(2)}, u32[]{:S(2)}) collective-permute-start(bf16[8,72,768]{2,1,0:T(8,128)(2,1)} %slice.120), channel_id=1, source_target_pairs={{0,28},{4,0},{8,4},{12,8},{16,12},{20,16},{24,20},{28,24},{1,29},{... | collective-permute-start | bytes 2654216 | tf_op jit(solution)/shard_map/ppermute | solution.py:597
  225.1 6.6 %collective-permute-start = (bf16[16,8,768]{2,1,0:T(8,128)(2,1)}, bf16[16,8,768]{2,1,0:T(8,128)(2,1)}, u32[]{:S(2)}, u32[]{:S(2)}) collective-permute-start(bf16[16,8,768]{2,1,0:T(8,128)(2,1)} %slice.99), channel_id=1, source_target_pairs={{0,3},{1,0},{2,1},{3,2},{4,7},{5,4},{6,5},{7,6},{8,11},{9,8},{10,9... | collective-permute-start | bytes 589832 | tf_op jit(solution)/shard_map/ppermute | solution.py:597
  251.3 24.2 %all-to-all-start.8 = ((bf16[4,4,64,256]{3,2,1,0:T(8,128)(2,1)}), bf16[4,4,64,256]{3,2,1,0:T(8,128)(2,1)S(1)}, u32[]{:S(2)}, u32[]{:S(2)}) async-start(bf16[4,4,64,256]{3,2,1,0:T(8,128)(2,1)} %bitcast.96), calls=%async_computation.8 | async-start | bytes 1048576 | tf_op jit(solution)/shard_map/all_to_all | solution.py:367
  258.5 23.2 %copy-start.25 = (bf16[272,512]{1,0:T(8,128)(2,1)S(1)}, bf16[272,512]{1,0:T(8,128)(2,1)}, u32[]{:S(2)}) copy-start(bf16[272,512]{1,0:T(8,128)(2,1)} %constant.106.clone) | copy-start | bytes 835588
  275.6 11.4 %all-to-all-start.10 = ((bf16[4,4,64,256]{3,2,1,0:T(8,128)(2,1)}), bf16[4,4,64,256]{3,2,1,0:T(8,128)(2,1)S(1)}, u32[]{:S(2)}, u32[]{:S(2)}) async-start(bf16[4,4,64,256]{3,2,1,0:T(8,128)(2,1)} %bitcast.95), calls=%async_computation.10 | async-start | bytes 1048576 | tf_op jit(solution)/shard_map/all_to_all | solution.py:367
  286.9 31.6 %all-to-all-start.9 = ((bf16[32,2,64,128]{3,2,1,0:T(8,128)(2,1)}), bf16[32,2,64,128]{3,2,1,0:T(8,128)(2,1)S(1)}, u32[]{:S(2)}, u32[]{:S(2)}) async-start(bf16[32,2,64,128]{3,2,1,0:T(8,128)(2,1)} %bitcast.84), calls=%async_computation.9 | async-start | bytes 2097152 | tf_op jit(solution)/shard_map/all_to_all | solution.py:376
  318.6 30.8 %copy-start.4 = (bf16[32,2,64,128]{3,2,1,0:T(8,128)(2,1)}, bf16[32,2,64,128]{3,2,1,0:T(8,128)(2,1)S(1)}, u32[]{:S(2)}) copy-start(bf16[32,2,64,128]{3,2,1,0:T(8,128)(2,1)S(1)} %all-to-all-done.9.refs_0_) | copy-start | bytes 3145732
  318.6 29.9 %all-to-all-start.11 = ((bf16[32,2,64,128]{3,2,1,0:T(8,128)(2,1)}), bf16[32,2,64,128]{3,2,1,0:T(8,128)(2,1)S(1)}, u32[]{:S(2)}, u32[]{:S(2)}) async-start(bf16[32,2,64,128]{3,2,1,0:T(8,128)(2,1)} %bitcast.82), calls=%async_computation.11 | async-start | bytes 2097152 | tf_op jit(solution)/shard_map/all_to_all | solution.py:376
  363.4 33.4 %copy-start.22 = (bf16[16,64,256]{2,1,0:T(8,128)(2,1)S(1)}, bf16[16,64,256]{2,1,0:T(8,128)(2,1)}, u32[]{:S(2)}) copy-start(bf16[16,64,256]{2,1,0:T(8,128)(2,1)} %get-tuple-element.34) | copy-start | bytes 1572868
  363.4 35.5 %copy-start.21 = (bf16[16,64,256]{2,1,0:T(8,128)(2,1)S(1)}, bf16[16,64,256]{2,1,0:T(8,128)(2,1)}, u32[]{:S(2)}) copy-start(bf16[16,64,256]{2,1,0:T(8,128)(2,1)} %get-tuple-element.35) | copy-start | bytes 1572868
  393.4 33.0 %all-to-all-start.14 = ((bf16[32,2,64,128]{3,2,1,0:T(8,128)(2,1)}), bf16[32,2,64,128]{3,2,1,0:T(8,128)(2,1)S(1)}, u32[]{:S(2)}, u32[]{:S(2)}) async-start(bf16[32,2,64,128]{3,2,1,0:T(8,128)(2,1)} %get-tuple-element.41), calls=%async_computation.14 | async-start | bytes 2097152 | tf_op jit(solution)/shard_map/all_to_all | solution.py:399
  396.8 12.7 %collective-permute-start.3 = (bf16[16,8,256]{2,1,0:T(8,128)(2,1)S(1)}, bf16[16,8,256]{2,1,0:T(8,128)(2,1)S(1)}, u32[]{:S(2)}, u32[]{:S(2)}) collective-permute-start(bf16[16,8,256]{2,1,0:T(8,128)(2,1)S(1)} %slice.104), channel_id=1, source_target_pairs={{0,1},{1,2},{2,3},{3,0},{4,5},{5,6},{6,7},{7,4},{8,9},{9,10},{10,1... | collective-permute-start | bytes 196616 | tf_op jit(solution)/shard_map/ppermute | solution.py:597
  398.9 14.6 %collective-permute-start.5 = (bf16[16,8,256]{2,1,0:T(8,128)(2,1)S(1)}, bf16[16,8,256]{2,1,0:T(8,128)(2,1)S(1)}, u32[]{:S(2)}, u32[]{:S(2)}) collective-permute-start(bf16[16,8,256]{2,1,0:T(8,128)(2,1)S(1)} %slice.107), channel_id=1, source_target_pairs={{0,1},{1,2},{2,3},{3,0},{4,5},{5,6},{6,7},{7,4},{8,9},{9,10},{10,1... | collective-permute-start | bytes 196616 | tf_op jit(solution)/shard_map/ppermute | solution.py:597
  410.6 20.4 %collective-permute-start.4 = (bf16[8,72,256]{2,1,0:T(8,128)(2,1)}, bf16[8,72,256]{2,1,0:T(8,128)(2,1)}, u32[]{:S(2)}, u32[]{:S(2)}) collective-permute-start(bf16[8,72,256]{2,1,0:T(8,128)(2,1)} %slice.121), channel_id=1, source_target_pairs={{0,4},{4,8},{8,12},{12,16},{16,20},{20,24},{24,28},{28,0},{1,5},{5... | collective-permute-start | bytes 884744 | tf_op jit(solution)/shard_map/ppermute | solution.py:597
  426.4 12.1 %all-to-all-start.13 = ((bf16[4,4,64,256]{3,2,1,0:T(8,128)(2,1)}), bf16[4,4,64,256]{3,2,1,0:T(8,128)(2,1)S(1)}, u32[]{:S(2)}, u32[]{:S(2)}) async-start(bf16[4,4,64,256]{3,2,1,0:T(8,128)(2,1)} %shard_map.251), calls=%async_computation.13 | async-start | bytes 1048576 | tf_op jit(solution)/shard_map/all_to_all | solution.py:405
  438.5 29.2 %all-to-all-start.15 = ((bf16[4,4,64,256]{3,2,1,0:T(8,128)(2,1)}), bf16[4,4,64,256]{3,2,1,0:T(8,128)(2,1)S(1)}, u32[]{:S(2)}, u32[]{:S(2)}) async-start(bf16[4,4,64,256]{3,2,1,0:T(8,128)(2,1)} %shard_map.253), calls=%async_computation.15 | async-start | bytes 1048576 | tf_op jit(solution)/shard_map/all_to_all | solution.py:405
  458.6 5.5 collective-permute-start.7
  465.0 26.5 %collective-permute-start.8 = (bf16[8,72,512]{2,1,0:T(8,128)(2,1)}, bf16[8,72,512]{2,1,0:T(8,128)(2,1)S(1)}, u32[]{:S(2)}, u32[]{:S(2)}) collective-permute-start(bf16[8,72,512]{2,1,0:T(8,128)(2,1)} %slice.124), channel_id=1, source_target_pairs={{0,28},{4,0},{8,4},{12,8},{16,12},{20,16},{24,20},{28,24},{1,29},{... | collective-permute-start | bytes 1769480 | tf_op jit(solution)/shard_map/ppermute | solution.py:597
  484.5 7.1 %collective-permute-start.6 = (bf16[16,8,512]{2,1,0:T(8,128)(2,1)S(1)}, bf16[16,8,512]{2,1,0:T(8,128)(2,1)S(1)}, u32[]{:S(2)}, u32[]{:S(2)}) collective-permute-start(bf16[16,8,512]{2,1,0:T(8,128)(2,1)S(1)} %slice.110), channel_id=1, source_target_pairs={{0,3},{1,0},{2,1},{3,2},{4,7},{5,4},{6,5},{7,6},{8,11},{9,8},{10,9... | collective-permute-start | bytes 393224 | tf_op jit(solution)/shard_map/ppermute | solution.py:597
  510.2 5.6 %collective-permute-start.9 = (bf16[16,8,256]{2,1,0:T(8,128)(2,1)S(1)}, bf16[16,8,256]{2,1,0:T(8,128)(2,1)S(1)}, u32[]{:S(2)}, u32[]{:S(2)}) collective-permute-start(bf16[16,8,256]{2,1,0:T(8,128)(2,1)S(1)} %slice.125), channel_id=1, source_target_pairs={{0,1},{1,2},{2,3},{3,0},{4,5},{5,6},{6,7},{7,4},{8,9},{9,10},{10,1... | collective-permute-start | bytes 196616 | tf_op jit(solution)/shard_map/ppermute | solution.py:597
  516.8 24.1 %collective-permute-start.10 = (bf16[8,72,256]{2,1,0:T(8,128)(2,1)S(1)}, bf16[8,72,256]{2,1,0:T(8,128)(2,1)S(1)}, u32[]{:S(2)}, u32[]{:S(2)}) collective-permute-start(bf16[8,72,256]{2,1,0:T(8,128)(2,1)S(1)} %pad_maximum_fusion.9), channel_id=1, source_target_pairs={{0,4},{4,8},{8,12},{12,16},{16,20},{20,24},{24,28},{28,0},{1,5},{5... | collective-permute-start | bytes 884744 | tf_op jit(solution)/shard_map/ppermute | solution.py:597
  518.3 22.6 %copy-start.2 = (bf16[16,64,256]{2,1,0:T(8,128)(2,1)S(1)}, bf16[16,64,256]{2,1,0:T(8,128)(2,1)}, u32[]{:S(2)}) copy-start(bf16[16,64,256]{2,1,0:T(8,128)(2,1)} %shard_map.255) | copy-start | bytes 1572868
  518.3 22.6 %copy-start.19 = (f32[16,64,256]{2,1,0:T(8,128)S(1)}, f32[16,64,256]{2,1,0:T(8,128)}, u32[]{:S(2)}) copy-start(f32[16,64,256]{2,1,0:T(8,128)} %get-tuple-element.39) | copy-start | bytes 3145732
  518.3 22.6 %copy-start.20 = (f32[16,64,256]{2,1,0:T(8,128)S(1)}, f32[16,64,256]{2,1,0:T(8,128)}, u32[]{:S(2)}) copy-start(f32[16,64,256]{2,1,0:T(8,128)} %get-tuple-element.44) | copy-start | bytes 3145732
  535.7 5.2 collective-permute-start.11
  (21 other events, 99.6 us)
